TPU v7x, 32 devices: a whole 2x2x4 slice. The times are simulated.
32 devices in a mesh: dp: 2 (over x), context: 4 (over y, core), expert: 4 (over z).
Axes of the slice: x: 2, y: 2, z: 4, core: 2. Of those that a mesh axis runs over, the one named last changes fastest.
Arguments:
- tokens: bfloat16 [8, 1024, 1536], P(('dp', 'expert'), 'context'), may hold values from -6 to 6
- lengths: int32 [8], P(('dp', 'expert')), may hold values from 769 to 1024, as said below
- routes: int32 [8, 1024, 8], P(('dp', 'expert'), 'context'), may hold values from 0 to 31, all different within a row; in each aligned block of 256 rows (0 to 255, 256 to 511, ..., all dimensions but the last counted through in order) at most 96 rows name the same one
- gain_attn: bfloat16 [1536], P(('dp', 'context', 'expert')), may hold values from 0.5 to 1.5
- w_query: bfloat16 [1536, 1536], P(('dp', 'context', 'expert')), may hold values from -0.15625 to 0.15625
- key_weight: bfloat16 [1536, 512], P(('dp', 'context', 'expert')), may hold values from -0.15625 to 0.15625
- value_weight: bfloat16 [1536, 512], P(('dp', 'context', 'expert')), may hold values from -0.15625 to 0.15625
- w_out: bfloat16 [1536, 1536], P(('dp', 'context', 'expert')), may hold values from -1.25 to 1.25
- gain_ffn: bfloat16 [1536], P(('dp', 'context', 'expert')), may hold values from 0.5 to 1.5
- w_router: bfloat16 [1536, 32], P(('dp', 'context', 'expert')), may hold values from -0.078125 to 0.078125
- w_gate: bfloat16 [32, 1536, 512], P(('context', 'expert')), may hold values from -0.15625 to 0.15625
- w_up: bfloat16 [32, 1536, 512], P(('context', 'expert')), may hold values from -0.15625 to 0.15625
- w_down: bfloat16 [32, 512, 1536], P(('context', 'expert')), may hold values from -0.75 to 0.75
- cotangent: bfloat16 [8, 1024, 1536], P(('dp', 'expert'), 'context'), may hold values from -6 to 6
Outputs:
- block_out: bfloat16 [8, 1024, 1536], P(('dp', 'expert'), 'context')
- grad_tokens: float32 [8, 1024, 1536], P(('dp', 'expert'), 'context')
- grad_gain_attn: float32 [1536], P(('dp', 'context', 'expert'))
- grad_w_query: float32 [1536, 1536], P(('dp', 'context', 'expert'))
- grad_w_key: float32 [1536, 512], P(('dp', 'context', 'expert'))
- grad_w_value: float32 [1536, 512], P(('dp', 'context', 'expert'))
- grad_w_out: float32 [1536, 1536], P(('dp', 'context', 'expert'))
- grad_gain_ffn: float32 [1536], P(('dp', 'context', 'expert'))
- grad_w_router: float32 [1536, 32], P(('dp', 'context', 'expert'))
- grad_w_gate: float32 [32, 1536, 512], P(('context', 'expert'), 'dp')
- grad_w_up: float32 [32, 1536, 512], P(('context', 'expert'), 'dp')
- grad_w_down: float32 [32, 512, 1536], P(('context', 'expert'), 'dp')
Inputs may be any that keep to these rules, and one draw needn't show every extreme that they name: Within each aligned block of 256 positions of one slot, no expert is named by more than 96 of the block's routes. `lengths`: among the 1 consecutive slots that one index of dp and expert holds, one slot, drawn from the seed, is longer than 768; among the slots of one index of dp, one of these, drawn from the seed, has the full length 1024.
All inputs are finite; a program needn't handle non-finite values.
Results may differ from a plain program's by a relative error of at most 0.018.
Values may be sent and summed in bfloat16 or wider, within the bound.
A program may use at most 256 MiB of HBM per device.

v0:
```python
import functools
import math

import jax
import jax.numpy as jnp
from jax import lax
from jax.experimental import pallas as pl
from jax.experimental.pallas import tpu as pltpu
from jax.sharding import PartitionSpec as P

MODEL_WIDTH = 1536
HEAD_SIZE = 64
TOP = 8
epsilon = 1e-05
floor_score = -1e30


def rotation_tables(positions):
    half_size = HEAD_SIZE // 2
    exponent = jnp.arange(half_size, dtype=jnp.int32).astype(jnp.float32) * (2.0 / HEAD_SIZE)
    frequency = jnp.exp(-math.log(10000.0) * exponent)
    angles = frequency[:, None] * positions.astype(jnp.float32)[None, :]
    return (jnp.cos(angles), jnp.sin(angles))


def apply_rotation(values, cosine, sine):
    split = values.reshape(-1, 2, HEAD_SIZE // 2, values.shape[1])
    first = split[:, 0]
    second = split[:, 1]
    turned = jnp.stack([first * cosine - second * sine, second * cosine + first * sine], axis=1)
    return turned.reshape(values.shape)


def inverse_rotation(gradient, cosine, sine):
    return apply_rotation(gradient, cosine, -sine)


def norm_back(gradient, normed, inverse):
    return inverse * (gradient - normed * jnp.mean(gradient * normed, axis=-1, keepdims=True))


GROUP = ("context", "expert")
EVERY = ("dp", "context", "expert")


MESH_ID = pl.DeviceIdType.MESH
CHUNK = 512
HALF = 256
UP, DOWN, ACROSS, CORE, DP = 0, 1, 2, 3, 4


def contract_rows(left, right):
    return lax.dot_general(left, right, (((0,), (0,)), ((), ())), preferred_element_type=jnp.float32)


def contract_last(left, right):
    return lax.dot_general(left, right, (((1,), (1,)), ((), ())), preferred_element_type=jnp.float32)


def matmul(left, right):
    return jnp.dot(left, right, preferred_element_type=jnp.float32)


def line_order(z, step):
    half = z // 2
    inner = z + half * (3 - 2 * z)
    base = step + inner * (1 - 2 * step) * (1 - step // 2)
    return base + half * (3 - 2 * base)


def place():
    ctx = lax.axis_index("context")
    z = lax.axis_index("expert")
    y = ctx // 2
    c = ctx % 2
    inner = z + (z // 2) * (3 - 2 * z)

    def device(kind):
        if kind == UP:
            return {"context": ctx, "expert": z + 1}
        if kind == DOWN:
            return {"context": ctx, "expert": z - 1}
        if kind == ACROSS:
            return {"context": (1 - y) * 2 + c, "expert": z}
        if kind == CORE:
            return {"context": y * 2 + 1 - c, "expert": z}
        return {"dp": 1 - lax.axis_index("dp")}

    def per_side(action, more=()):
        @pl.when(z < 3)
        def _():
            action(UP)

        @pl.when(z > 0)
        def _():
            action(DOWN)

        for kind in (ACROSS, CORE, *more):
            action(kind)

    return y, c, z, inner, device, per_side


def block_id(yy, cc, zz):
    return (yy * 2 + cc) * 4 + zz


def greet(per_side, device, count, more=()):
    barrier = pltpu.get_barrier_semaphore()
    per_side(
        lambda kind: pl.semaphore_signal(
            barrier, inc=1, device_id=device(kind), device_id_type=MESH_ID
        ),
        more,
    )
    pl.semaphore_wait(barrier, count)


def swap_copies(pieces, device, send_sem, recv_sem):
    d = lax.axis_index("dp")
    copies = []
    for index, (source, j, target) in enumerate(pieces):
        half = target.shape[0]
        copies.append(
            pltpu.make_async_remote_copy(
                src_ref=source.at[j, pl.ds(pl.multiple_of((1 - d) * half, 128), half), :],
                dst_ref=target,
                send_sem=send_sem.at[index],
                recv_sem=recv_sem.at[index],
                device_id=device(DP),
                device_id_type=MESH_ID,
            )
        )
    return copies


def ring_sum(parts, core_got, y_got, z_got, dp_got, sems):
    single = jnp.float32
    core_send, core_recv, y_send, y_recv, z_send, z_recv, dp_send, dp_recv = sems
    y, c, z, _, device, _ = place()
    d = lax.axis_index("dp")
    rows = parts.shape[1] // 2
    mine = block_id(y, c, z)

    def remote(kind, source, target, send_sem, recv_sem):
        return pltpu.make_async_remote_copy(
            src_ref=source,
            dst_ref=target,
            send_sem=send_sem,
            recv_sem=recv_sem,
            device_id=device(kind),
            device_id_type=MESH_ID,
        )

    def to_core(yy, zz):
        slot = yy * 4 + zz
        return remote(
            CORE, parts.at[block_id(yy, 1 - c, zz)], core_got.at[slot], core_send.at[slot], core_recv.at[slot]
        )

    def to_across(zz):
        return remote(ACROSS, parts.at[block_id(1 - y, c, zz)], y_got.at[zz], y_send.at[zz], y_recv.at[zz])

    def to_line(kind, zz, slot):
        return remote(kind, parts.at[block_id(y, c, zz)], z_got.at[slot], z_send.at[zz], z_recv.at[slot])

    def add(block, got):
        parts[block] = (parts[block].astype(single) + got.astype(single)).astype(parts.dtype)

    def core_sends():
        @pl.loop(0, 4)
        def _(turn):
            zz = line_order(z, 3 - turn)
            to_core(1 - y, zz).start()
            to_core(y, zz).start()

    def across(step):
        zz = line_order(z, step)
        to_core(1 - y, zz).wait_recv()
        add(block_id(1 - y, c, zz), core_got[(1 - y) * 4 + zz])
        to_across(zz).start()
        to_core(y, zz).wait_recv()
        add(block_id(y, c, zz), core_got[y * 4 + zz])

    def line(step):
        zz = line_order(z, step)
        block = block_id(y, c, zz)
        to_across(zz).wait_recv()
        add(block, y_got[zz])
        rising = zz > z
        comes = jnp.logical_or(jnp.logical_and(rising, z > 0), jnp.logical_and(zz < z, z < 3))

        @pl.when(comes)
        def _():
            to_line(CORE, zz, zz).wait_recv()
            add(block, z_got[zz])

        @pl.when(rising)
        def _():
            to_line(UP, zz, zz).start()

        @pl.when(zz == z - 1)
        def _():
            to_line(DOWN, zz, 4).start()

        @pl.when(zz < z - 1)
        def _():
            to_line(DOWN, zz, zz).start()

    there = pl.ds(pl.multiple_of((1 - d) * rows, 16), rows)
    here = pl.ds(pl.multiple_of(d * rows, 16), rows)
    last = remote(DP, parts.at[mine, there, :], dp_got, dp_send, dp_recv)

    def over_dp():
        to_across(z).wait_recv()
        add(mine, y_got[z])

        @pl.when(z > 0)
        def _():
            to_line(CORE, z, z).wait_recv()
            add(mine, z_got[z])

        @pl.when(z < 3)
        def _():
            to_line(CORE, z, 4).wait_recv()
            add(mine, z_got[4])

        last.start()

    def finish(result):
        last.wait_recv()
        result[...] = parts[mine, here, :].astype(single) + dp_got[...].astype(single)
        last.wait_send()

        @pl.loop(0, 4)
        def _(zz):
            to_core(y, zz).wait_send()
            to_core(1 - y, zz).wait_send()
            to_across(zz).wait_send()

            @pl.when(zz != z)
            def _():
                to_line(CORE, zz, zz).wait_send()

    return core_sends, across, line, over_dp, finish


def ring_scratch(rows, width):
    bfloat = jnp.bfloat16
    dma = pltpu.SemaphoreType.DMA
    return [
        pltpu.VMEM((16, 2 * rows, width), bfloat),
        pltpu.VMEM((8, 2 * rows, width), bfloat),
        pltpu.VMEM((4, 2 * rows, width), bfloat),
        pltpu.VMEM((5, 2 * rows, width), bfloat),
        pltpu.VMEM((rows, width), bfloat),
        dma((8,)),
        dma((8,)),
        dma((4,)),
        dma((4,)),
        dma((4,)),
        dma((5,)),
        dma,
        dma,
    ]


def load_parts(refs, parts, sem):
    loads = []
    at = 0
    for index, ref in enumerate(refs):
        rows, size = ref.shape[2], ref.shape[3]
        for plane in range(2):
            loads.append(
                pltpu.make_async_copy(
                    ref.at[plane],
                    parts.at[:, pl.ds(plane * rows, rows), pl.ds(at, size)],
                    sem.at[index * 2 + plane],
                )
            )
        at += size
    return loads


def spread_rows(whole, send_sem, core_sem, recv_sem):
    y, c, z, _, device, _ = place()
    d = lax.axis_index("dp")

    def copy_of(kind, slot, sem):
        return pltpu.make_async_remote_copy(
            src_ref=whole.at[slot],
            dst_ref=whole.at[slot],
            send_sem=sem,
            recv_sem=recv_sem.at[slot],
            device_id=device(kind),
            device_id_type=MESH_ID,
        )

    def own(kind, block):
        return copy_of(kind, d * 16 + block, send_sem.at[kind, block])

    def other(block):
        return copy_of(CORE, (1 - d) * 16 + block, core_sem.at[block])

    def along(kind, zz):
        if kind == UP:
            return jnp.logical_and(z < 3, zz <= z)
        return jnp.logical_and(z > 0, zz >= z)

    def fan(zz, act):
        block = block_id(y, c, zz)
        for kind in (UP, DOWN):

            @pl.when(along(kind, zz))
            def _():
                act(own(kind, block))

        for kind in (ACROSS, DP, CORE):
            act(own(kind, block))

    def fan_across(zz, act):
        block = block_id(1 - y, c, zz)
        act(own(DP, block))
        act(own(CORE, block))

    def fan_dp(zz, act):
        act(other(block_id(y, c, zz)))
        act(other(block_id(1 - y, c, zz)))

    start = lambda copy: copy.start()
    end = lambda copy: copy.wait_send()

    def begin():
        fan(z, start)

    def arrive(step):
        @pl.when(step < 4)
        def _():
            zz = line_order(z, jnp.minimum(step, 3))
            own(ACROSS, block_id(y, c, zz)).wait_recv()
            fan(zz, start)

        @pl.when(step < 5)
        def _():
            zz = line_order(z, jnp.minimum(step - 1, 3))
            own(CORE, block_id(1 - y, c, zz)).wait_recv()
            fan_across(zz, start)

        @pl.when(step > 1)
        def _():
            zz = line_order(z, jnp.maximum(step - 2, 0))
            other(block_id(y, c, zz)).wait_recv()
            other(block_id(1 - y, c, zz)).wait_recv()
            fan_dp(zz, start)

    def finish():
        @pl.loop(0, 4)
        def _(zz):
            for yy in range(2):
                block = block_id(yy, 1 - c, zz)
                own(CORE, block).wait_recv()
                other(block).wait_recv()

    def ends():
        @pl.loop(0, 4)
        def _(zz):
            fan(zz, end)
            fan_across(zz, end)
            fan_dp(zz, end)

    return begin, arrive, finish, ends


def spread_scratch(rows, width):
    dma = pltpu.SemaphoreType.DMA
    return [pltpu.VMEM((32, rows, width), jnp.bfloat16), dma((5, 16)), dma((16,)), dma((32,))]


def gather_kernel(
    query_ref,
    key_ref,
    value_ref,
    small_ref,
    out_ref,
    proj_all,
    small_all,
    out_all,
    local_sem,
    whole,
    *sems,
):
    y, c, z, inner, device, per_side = place()
    mine = lax.axis_index("dp") * 16 + block_id(y, c, z)
    loads = []
    at = 0
    for index, ref in enumerate((query_ref, key_ref, value_ref, small_ref, out_ref)):
        size = ref.shape[1]
        loads.append(
            pltpu.make_async_copy(ref, whole.at[mine, :, pl.ds(at, size)], local_sem.at[index])
        )
        at += size
    for copy in loads:
        copy.start()
    greet(per_side, device, 4 + inner, (DP,))
    for copy in loads:
        copy.wait()
    begin, arrive, finish, ends = spread_rows(whole, *sems)
    begin()

    @pl.loop(1, 6)
    def _(step):
        arrive(step)

    finish()
    results = []
    at = 0
    for index, ref in enumerate((proj_all, small_all, out_all)):
        size = ref.shape[2]
        results.append(
            pltpu.make_async_copy(whole.at[:, :, pl.ds(at, size)], ref, local_sem.at[index])
        )
        at += size
    for copy in results:
        copy.start()
    ends()
    for copy in results:
        copy.wait()


def gather_weights(query, key, value, small, out):
    rows = query.shape[0]
    widths = (query.shape[1] + key.shape[1] + value.shape[1], small.shape[1], out.shape[1])
    anywhere = pl.BlockSpec(memory_space=pl.ANY)
    return pl.pallas_call(
        gather_kernel,
        out_shape=tuple(
            jax.ShapeDtypeStruct((32, rows, width), jnp.bfloat16) for width in widths
        ),
        in_specs=[anywhere] * 5,
        out_specs=(anywhere, anywhere, anywhere),
        scratch_shapes=[pltpu.SemaphoreType.DMA((5,)), *spread_scratch(rows, sum(widths))],
        compiler_params=pltpu.CompilerParams(
            collective_id=0, has_side_effects=True, vmem_limit_bytes=60 * 2**20
        ),
        name="gather_weights",
    )(query, key, value, small, out)


def ring_sum_dp_early(parts, core_got, dp_got, y_got, z_got, sems):
    single = jnp.float32
    core_send, core_recv, dp_send, dp_recv, y_send, y_recv, z_send, z_recv = sems
    y, c, z, _, device, _ = place()
    d = lax.axis_index("dp")
    rows = parts.shape[1] // 2
    mine = block_id(y, c, z)
    there = pl.ds(pl.multiple_of((1 - d) * rows, 16), rows)
    here = pl.ds(pl.multiple_of(d * rows, 16), rows)

    def remote(kind, source, target, send_sem, recv_sem):
        return pltpu.make_async_remote_copy(
            src_ref=source,
            dst_ref=target,
            send_sem=send_sem,
            recv_sem=recv_sem,
            device_id=device(kind),
            device_id_type=MESH_ID,
        )

    def to_core(yy, zz):
        slot = yy * 4 + zz
        return remote(
            CORE, parts.at[block_id(yy, 1 - c, zz)], core_got.at[slot], core_send.at[slot], core_recv.at[slot]
        )

    def to_dp(yy, zz):
        slot = yy * 4 + zz
        return remote(
            DP, parts.at[block_id(yy, c, zz), there, :], dp_got.at[slot], dp_send.at[slot], dp_recv.at[slot]
        )

    def to_across(zz):
        return remote(
            ACROSS, parts.at[block_id(1 - y, c, zz), here, :], y_got.at[zz], y_send.at[zz], y_recv.at[zz]
        )

    def to_line(kind, zz, slot):
        return remote(
            kind, parts.at[block_id(y, c, zz), here, :], z_got.at[slot], z_send.at[zz], z_recv.at[slot]
        )

    def add(block, got):
        parts[block, here, :] = (
            parts[block, here, :].astype(single) + got.astype(single)
        ).astype(parts.dtype)

    def core_sends():
        @pl.loop(0, 4)
        def _(turn):
            zz = line_order(z, 3 - turn)
            to_core(1 - y, zz).start()
            to_core(y, zz).start()

    def meet(step):
        zz = line_order(z, step)
        for yy in (1 - y, y):
            block = block_id(yy, c, zz)
            to_core(yy, zz).wait_recv()
            parts[block] = (
                parts[block].astype(single) + core_got[yy * 4 + zz].astype(single)
            ).astype(parts.dtype)
            to_dp(yy, zz).start()

    def across(step):
        zz = line_order(z, step)
        for yy in (1 - y, y):
            to_dp(yy, zz).wait_recv()
            add(block_id(yy, c, zz), dp_got[yy * 4 + zz])
        to_across(zz).start()

    def line(step):
        zz = line_order(z, step)
        block = block_id(y, c, zz)
        to_across(zz).wait_recv()
        add(block, y_got[zz])
        rising = zz > z
        comes = jnp.logical_or(jnp.logical_and(rising, z > 0), jnp.logical_and(zz < z, z < 3))

        @pl.when(comes)
        def _():
            to_line(CORE, zz, zz).wait_recv()
            add(block, z_got[zz])

        @pl.when(rising)
        def _():
            to_line(UP, zz, zz).start()

        @pl.when(zz == z - 1)
        def _():
            to_line(DOWN, zz, 4).start()

        @pl.when(zz < z - 1)
        def _():
            to_line(DOWN, zz, zz).start()

    def finish(results):
        spans = []
        at = 0
        for result in results:
            spans.append(pl.ds(at, result.shape[1]))
            at += result.shape[1]
        to_across(z).wait_recv()
        for result, span in zip(results, spans):
            result[...] = parts[mine, here, span].astype(single) + y_got[z, :, span].astype(single)

        @pl.when(z > 0)
        def _():
            to_line(CORE, z, z).wait_recv()
            for result, span in zip(results, spans):
                result[...] += z_got[z, :, span].astype(single)

        @pl.when(z < 3)
        def _():
            to_line(CORE, z, 4).wait_recv()
            for result, span in zip(results, spans):
                result[...] += z_got[4, :, span].astype(single)

        @pl.loop(0, 4)
        def _(zz):
            for yy in (y, 1 - y):
                to_core(yy, zz).wait_send()
                to_dp(yy, zz).wait_send()
            to_across(zz).wait_send()

            @pl.when(zz != z)
            def _():
                to_line(CORE, zz, zz).wait_send()

    return core_sends, meet, across, line, finish


def ring_scratch_dp_early(rows, width):
    bfloat = jnp.bfloat16
    dma = pltpu.SemaphoreType.DMA
    return [
        pltpu.VMEM((16, 2 * rows, width), bfloat),
        pltpu.VMEM((8, 2 * rows, width), bfloat),
        pltpu.VMEM((8, rows, width), bfloat),
        pltpu.VMEM((4, rows, width), bfloat),
        pltpu.VMEM((5, rows, width), bfloat),
        *[dma((n,)) for n in (8, 8, 8, 8, 4, 4, 4, 5)],
    ]


def sums_kernel(
    proj_ref, small_ref, out_ref, query_sum, key_sum, value_sum, small_sum, out_sum, load_sem, *rings
):
    _, _, _, inner, device, per_side = place()
    ring, out_ring = rings[:13], rings[13:]
    loads = load_parts((proj_ref, small_ref), ring[0], load_sem) + load_parts(
        (out_ref,), out_ring[0], load_sem.at[pl.ds(4, 2)]
    )
    for copy in loads:
        copy.start()
    greet(per_side, device, 4 + inner, (DP,))
    for copy in loads:
        copy.wait()
    core_sends, meet, across, line, finish = ring_sum_dp_early(*ring[:5], ring[5:])
    out_core, out_across, out_line, out_dp, out_finish = ring_sum(*out_ring[:5], out_ring[5:])
    core_sends()
    out_core()

    @pl.loop(0, 4)
    def _(turn):
        meet(3 - turn)
        out_across(3 - turn)

    @pl.loop(0, 4)
    def _(turn):
        across(3 - turn)

        @pl.when(turn < 3)
        def _():
            out_line(3 - jnp.minimum(turn, 2))

        @pl.when(turn > 0)
        def _():
            line(4 - jnp.maximum(turn, 1))

    out_dp()
    finish((query_sum, key_sum, value_sum, small_sum))
    out_finish(out_sum)


def by_device(x):
    return x.reshape(2, 16, x.shape[0] // 32, x.shape[1])


def sum_gradients(proj, small, out, widths):
    dma = pltpu.SemaphoreType.DMA
    anywhere = pl.BlockSpec(memory_space=pl.ANY)
    vmem = pl.BlockSpec(memory_space=pltpu.VMEM)
    rows = proj.shape[0] // 32
    width = proj.shape[1] + small.shape[1]
    return pl.pallas_call(
        sums_kernel,
        out_shape=(
            *(jax.ShapeDtypeStruct((rows, size), jnp.float32) for size in widths),
            jax.ShapeDtypeStruct((rows, small.shape[1]), jnp.float32),
            jax.ShapeDtypeStruct((rows, out.shape[1]), jnp.float32),
        ),
        in_specs=[anywhere] * 3,
        out_specs=(vmem,) * (2 + len(widths)),
        scratch_shapes=[
            dma((6,)),
            *ring_scratch_dp_early(rows, width),
            *ring_scratch(rows, out.shape[1]),
        ],
        compiler_params=pltpu.CompilerParams(
            collective_id=2, has_side_effects=True, vmem_limit_bytes=56 * 2**20
        ),
        cost_estimate=pl.CostEstimate(flops=1 << 20, bytes_accessed=1 << 16, transcendentals=0),
        name="sum_gradients",
    )(by_device(proj), by_device(small), by_device(out))


def fill_bias(length_ref, bias, ctx):
    blocks, keys, queries = bias.shape
    row = lax.broadcasted_iota(jnp.int32, (keys, queries), 0)
    column = lax.broadcasted_iota(jnp.int32, (keys, queries), 1) + ctx * queries
    for j in range(blocks):
        key = row + j * keys
        allowed = jnp.logical_and(key <= column, key < length_ref[0])
        bias[j] = jnp.where(allowed, 0.0, floor_score)


def head_probs(query, keys, bias):
    scores = [contract_rows(key, query) + bias[j] for j, key in enumerate(keys)]
    peak = jnp.max(scores[0], axis=0, keepdims=True)
    for score in scores[1:]:
        peak = jnp.maximum(peak, jnp.max(score, axis=0, keepdims=True))
    raised = [jnp.exp(score - peak) for score in scores]
    total = jnp.sum(raised[0], axis=0, keepdims=True)
    for value in raised[1:]:
        total = total + jnp.sum(value, axis=0, keepdims=True)
    inverse = 1.0 / total
    return [value * inverse for value in raised]


def attend_kernel(
    query_ref,
    own_ref,
    length_ref,
    mixed_ref,
    all_ref,
    pairs,
    bias,
    first,
    stats,
    local_sem,
    send_sem,
    recv_sem,
):
    bfloat = jnp.bfloat16
    y, c, _, _, device, _ = place()
    mine = y * 2 + c
    own = pltpu.make_async_copy(own_ref, pairs.at[mine], local_sem)
    own.start()
    barrier = pltpu.get_barrier_semaphore()
    for kind in (ACROSS, CORE):
        pl.semaphore_signal(barrier, inc=1, device_id=device(kind), device_id_type=MESH_ID)
    pl.semaphore_wait(barrier, 2)
    own.wait()

    def send(kind, slot, index):
        return pltpu.make_async_remote_copy(
            src_ref=pairs.at[slot],
            dst_ref=pairs.at[slot],
            send_sem=send_sem.at[index],
            recv_sem=recv_sem.at[slot],
            device_id=device(kind),
            device_id_type=MESH_ID,
        )

    far = (1 - y) * 2 + c
    across = send(ACROSS, mine, 0)
    core = send(CORE, mine, 1)
    onward = send(CORE, far, 2)
    across.start()
    core.start()
    fill_bias(length_ref, bias, mine)
    half = pairs.shape[1] // 2
    ratio = query_ref.shape[0] // half
    groups = half // HEAD_SIZE

    def pass_over(blocks, g, merge):
        rows = pl.ds(pl.multiple_of(g * HEAD_SIZE, HEAD_SIZE), HEAD_SIZE)
        low = pl.ds(pl.multiple_of(half + g * HEAD_SIZE, HEAD_SIZE), HEAD_SIZE)
        keys = [pairs[j, rows, :] for j in blocks]
        values = [pairs[j, low, :] for j in blocks]
        for r in range(ratio):
            h = g * ratio + r
            head = pl.ds(pl.multiple_of(h * HEAD_SIZE, HEAD_SIZE), HEAD_SIZE)
            query = query_ref[head, :]
            scores = [contract_rows(key, query) + bias[j] for key, j in zip(keys, blocks)]
            peak = jnp.maximum(
                jnp.max(scores[0], axis=0, keepdims=True), jnp.max(scores[1], axis=0, keepdims=True)
            )
            if merge:
                before = stats[h, 0:1, :]
                peak = jnp.maximum(peak, before)
            raised = [jnp.exp(score - peak) for score in scores]
            total = jnp.sum(raised[0] + raised[1], axis=0, keepdims=True)
            sums = matmul(values[0], raised[0].astype(bfloat)) + matmul(
                values[1], raised[1].astype(bfloat)
            )
            if merge:
                shrink = jnp.exp(before - peak)
                total = total + stats[h, 1:2, :] * shrink
                mixed_ref[head, :] = ((sums + first[head, :] * shrink) / total).astype(bfloat)
            else:
                first[head, :] = sums
                stats[h, 0:1, :] = peak
                stats[h, 1:2, :] = total

    send(CORE, y * 2 + 1 - c, 1).wait_recv()

    @pl.loop(0, groups)
    def _(g):
        pass_over((mine, y * 2 + 1 - c), g, False)

    send(ACROSS, far, 0).wait_recv()
    onward.start()
    send(CORE, (1 - y) * 2 + 1 - c, 2).wait_recv()
    result = pltpu.make_async_copy(pairs, all_ref, local_sem)
    result.start()

    @pl.loop(0, groups)
    def _(g):
        pass_over((far, (1 - y) * 2 + 1 - c), g, True)

    for copy in (across, core, onward):
        copy.wait_send()
    result.wait()


def attend(query, own_pairs, lengths):
    bfloat = jnp.bfloat16
    single = jnp.float32
    dma = pltpu.SemaphoreType.DMA
    anywhere = pl.BlockSpec(memory_space=pl.ANY)
    vmem = pl.BlockSpec(memory_space=pltpu.VMEM)
    pairs = (4, *own_pairs.shape)
    keys = own_pairs.shape[1]
    return pl.pallas_call(
        attend_kernel,
        out_shape=(
            jax.ShapeDtypeStruct(query.shape, bfloat),
            jax.ShapeDtypeStruct(pairs, bfloat),
        ),
        in_specs=[vmem, anywhere, pl.BlockSpec(memory_space=pltpu.SMEM)],
        out_specs=(vmem, anywhere),
        scratch_shapes=[
            pltpu.VMEM(pairs, bfloat),
            pltpu.VMEM((4, keys, query.shape[1]), single),
            pltpu.VMEM(query.shape, single),
            pltpu.VMEM((query.shape[0] // HEAD_SIZE, 8, query.shape[1]), single),
            dma,
            dma((3,)),
            dma((4,)),
        ],
        compiler_params=pltpu.CompilerParams(
            collective_id=3, has_side_effects=True, vmem_limit_bytes=48 * 2**20
        ),
        name="attend",
    )(query, own_pairs, lengths)


def turn_back(gradient, cosine, sine):
    first, second = gradient[: HEAD_SIZE // 2], gradient[HEAD_SIZE // 2 :]
    return jnp.concatenate(
        [first * cosine + second * sine, second * cosine - first * sine], axis=0
    ).astype(jnp.bfloat16)


def attend_back_kernel(
    query_ref,
    pairs_ref,
    grad_ref,
    length_ref,
    cosine_ref,
    sine_ref,
    proj_out,
    parts,
    core_got,
    y_got,
    bias,
    core_send,
    core_recv,
    y_send,
    y_recv,
):
    bfloat = jnp.bfloat16
    single = jnp.float32
    y, c, _, _, device, _ = place()
    mine = y * 2 + c
    barrier = pltpu.get_barrier_semaphore()
    for kind in (ACROSS, CORE):
        pl.semaphore_signal(barrier, inc=1, device_id=device(kind), device_id_type=MESH_ID)
    pl.semaphore_wait(barrier, 2)
    fill_bias(length_ref, bias, mine)
    blocks = pairs_ref.shape[0]
    half = pairs_ref.shape[1] // 2
    ratio = query_ref.shape[0] // half
    groups = half // HEAD_SIZE
    turns = parts.shape[1]
    per_turn = groups // turns
    quarter = half // turns

    def to_core(yy, turn):
        return pltpu.make_async_remote_copy(
            src_ref=parts.at[yy * 2 + 1 - c, turn],
            dst_ref=core_got.at[turn, yy],
            send_sem=core_send.at[turn, yy],
            recv_sem=core_recv.at[turn, yy],
            device_id=device(CORE),
            device_id_type=MESH_ID,
        )

    def to_across(turn):
        return pltpu.make_async_remote_copy(
            src_ref=parts.at[(1 - y) * 2 + c, turn],
            dst_ref=y_got.at[turn],
            send_sem=y_send.at[turn],
            recv_sem=y_recv.at[turn],
            device_id=device(ACROSS),
            device_id_type=MESH_ID,
        )

    def core_stage(turn):
        to_core(1 - y, turn).start()
        to_core(y, turn).start()

    def across_stage(turn):
        to_core(1 - y, turn).wait_recv()
        slot = (1 - y) * 2 + c
        parts[slot, turn] = (
            parts[slot, turn].astype(single) + core_got[turn, 1 - y].astype(single)
        ).astype(bfloat)
        to_across(turn).start()

    def last_stage(turn):
        to_core(y, turn).wait_recv()
        to_across(turn).wait_recv()
        total = (
            parts[mine, turn].astype(single)
            + core_got[turn, y].astype(single)
            + y_got[turn].astype(single)
        )
        at = query_ref.shape[0] + turn * quarter
        for h in range(per_turn):
            rows = slice(h * HEAD_SIZE, (h + 1) * HEAD_SIZE)
            proj_out[pl.ds(at + h * HEAD_SIZE, HEAD_SIZE), :] = turn_back(
                total[rows], cosine_ref[...], sine_ref[...]
            )
        proj_out[pl.ds(at + half, quarter), :] = total[quarter:].astype(bfloat)

    def group(g, carry):
        rows = pl.ds(pl.multiple_of(g * HEAD_SIZE, HEAD_SIZE), HEAD_SIZE)
        low = pl.ds(pl.multiple_of(half + g * HEAD_SIZE, HEAD_SIZE), HEAD_SIZE)
        keys = [pairs_ref[j, rows, :] for j in range(blocks)]
        values = [pairs_ref[j, low, :] for j in range(blocks)]
        grad_keys = [None] * blocks
        grad_values = [None] * blocks
        for r in range(ratio):
            head = pl.ds(pl.multiple_of((g * ratio + r) * HEAD_SIZE, HEAD_SIZE), HEAD_SIZE)
            query = query_ref[head, :]
            grad = grad_ref[head, :]
            probs = head_probs(query, keys, bias)
            grad_probs = [contract_rows(value, grad) for value in values]
            delta = jnp.sum(probs[0] * grad_probs[0], axis=0, keepdims=True)
            for j in range(1, blocks):
                delta = delta + jnp.sum(probs[j] * grad_probs[j], axis=0, keepdims=True)
            grad_query = None
            for j in range(blocks):
                low_probs = probs[j].astype(bfloat)
                grad_score = (probs[j] * (grad_probs[j] - delta)).astype(bfloat)
                terms = (
                    matmul(keys[j], grad_score),
                    contract_last(query, grad_score),
                    contract_last(grad, low_probs),
                )
                grad_query = terms[0] if j == 0 else grad_query + terms[0]
                grad_keys[j] = terms[1] if r == 0 else grad_keys[j] + terms[1]
                grad_values[j] = terms[2] if r == 0 else grad_values[j] + terms[2]
            proj_out[head, :] = turn_back(
                grad_query * HEAD_SIZE ** (-0.5), cosine_ref[...], sine_ref[...]
            )
        turn = g // per_turn
        at = pl.multiple_of((g % per_turn) * HEAD_SIZE, HEAD_SIZE)
        for j in range(blocks):
            parts[j, turn, pl.ds(at, HEAD_SIZE), :] = grad_keys[j].astype(bfloat)
            parts[j, turn, pl.ds(quarter + at, HEAD_SIZE), :] = grad_values[j].astype(bfloat)
        for index in range(turns - 1):

            @pl.when(g == (index + 1) * per_turn - 1)
            def _():
                core_stage(index)

            @pl.when(g == (index + 1) * per_turn)
            def _():
                across_stage(index)

        return carry

    lax.fori_loop(0, groups, group, 0)
    core_stage(turns - 1)
    across_stage(turns - 1)
    for turn in range(turns):
        last_stage(turn)
    for turn in range(turns):
        to_core(y, turn).wait_send()
        to_core(1 - y, turn).wait_send()
        to_across(turn).wait_send()


def attend_back(query, pairs, grad, lengths, cosine, sine):
    bfloat = jnp.bfloat16
    single = jnp.float32
    dma = pltpu.SemaphoreType.DMA
    anywhere = pl.BlockSpec(memory_space=pl.ANY)
    vmem = pl.BlockSpec(memory_space=pltpu.VMEM)
    blocks, rows, keys = pairs.shape
    turns = 4
    part = (turns, rows // turns, keys)
    return pl.pallas_call(
        attend_back_kernel,
        out_shape=jax.ShapeDtypeStruct((query.shape[0] + rows, query.shape[1]), bfloat),
        in_specs=[vmem, vmem, vmem, pl.BlockSpec(memory_space=pltpu.SMEM), vmem, vmem],
        out_specs=vmem,
        scratch_shapes=[
            pltpu.VMEM((blocks, *part), bfloat),
            pltpu.VMEM((turns, 2, *part[1:]), bfloat),
            pltpu.VMEM(part, bfloat),
            pltpu.VMEM((blocks, keys, query.shape[1]), single),
            dma((turns, 2)),
            dma((turns, 2)),
            dma((turns,)),
            dma((turns,)),
        ],
        compiler_params=pltpu.CompilerParams(
            collective_id=4, has_side_effects=True, vmem_limit_bytes=48 * 2**20
        ),
        cost_estimate=pl.CostEstimate(flops=1 << 20, bytes_accessed=1 << 16, transcendentals=0),
        name="attend_back",
    )(query, pairs, grad, lengths, cosine, sine)


def experts_kernel(
    swap,
    hidden_ref,
    final_ref,
    routes_ref,
    router_ref,
    gate_hbm,
    up_hbm,
    down_hbm,
    back_ref,
    part_ref,
    score_got,
    grad_gate_ref,
    grad_up_ref,
    grad_down_ref,
    *refs,
):
    if swap:
        gate_got, up_got, leaving, *refs = refs
        swap = (gate_got, up_got, leaving)
    experts_steps(
        swap,
        hidden_ref,
        final_ref,
        routes_ref,
        router_ref,
        gate_hbm,
        up_hbm,
        down_hbm,
        back_ref,
        part_ref,
        score_got,
        grad_gate_ref,
        grad_up_ref,
        grad_down_ref,
        *refs,
    )


def experts_steps(
    swap,
    hidden_ref,
    final_ref,
    routes_ref,
    router_ref,
    gate_hbm,
    up_hbm,
    down_hbm,
    back_ref,
    part_ref,
    score_got,
    grad_gate_ref,
    grad_up_ref,
    grad_down_ref,
    held,
    w_gate,
    w_up,
    w_down,
    rows_in,
    rows_grad,
    slope_gate,
    slope_up,
    hidden_e,
    picks,
    row_gates,
    work,
    pool,
    before,
    gather_send,
    gather_recv,
    local_sem,
    load_sem,
    part_sem,
    sum_send,
    core_recv,
    y_recv,
    z_recv,
    ready,
    score_ref,
    score_send,
    score_recv,
    swap_send,
    swap_recv,
):
    single = jnp.float32
    bfloat = jnp.bfloat16
    tokens_block = hidden_ref.shape[0]
    width = hidden_ref.shape[1]
    experts = router_ref.shape[0]
    local_exp = w_gate.shape[0]
    hidden_units = w_gate.shape[2]
    capacity = picks.shape[1] // local_exp
    group_rows = 4 * capacity
    ctx = lax.axis_index("context")
    y, c, z, inner, device, per_side = place()

    weights = (
        pltpu.make_async_copy(gate_hbm, w_gate, load_sem.at[0]),
        pltpu.make_async_copy(up_hbm, w_up, load_sem.at[1]),
        pltpu.make_async_copy(down_hbm, w_down, load_sem.at[2]),
    )
    mine = block_id(y, c, z)
    own = pltpu.make_async_copy(hidden_ref, held.at[mine], local_sem)
    own.start()
    for copy in weights:
        copy.start()

    barrier = pltpu.get_barrier_semaphore()

    def member_device(block):
        return {"context": block // 4, "expert": block % 4}

    @pl.loop(1, 16)
    def _(shift):
        pl.semaphore_signal(
            barrier,
            inc=1,
            device_id=member_device((mine + shift) % 16),
            device_id_type=MESH_ID,
        )

    if swap:
        pl.semaphore_signal(barrier, inc=1, device_id=device(DP), device_id_type=MESH_ID)
    pl.semaphore_wait(barrier, 16 if swap else 15)
    own.wait()

    def spread(kind, block):
        return pltpu.make_async_remote_copy(
            src_ref=held.at[block],
            dst_ref=held.at[block],
            send_sem=gather_send.at[kind, block],
            recv_sem=gather_recv.at[block],
            device_id=device(kind),
            device_id_type=MESH_ID,
        )

    def along(kind, zz):
        if kind == UP:
            return jnp.logical_and(z < 3, zz <= z)
        return jnp.logical_and(z > 0, zz >= z)

    def send_on(zz):
        block = block_id(y, c, zz)
        for kind in (UP, DOWN):

            @pl.when(along(kind, zz))
            def _():
                spread(kind, block).start()

        spread(ACROSS, block).start()
        spread(CORE, block).start()

    def forward(step):
        zz = line_order(z, step)
        spread(ACROSS, block_id(y, c, zz)).wait_recv()
        send_on(zz)

    send_on(z)
    row = lax.broadcasted_iota(jnp.int32, (tokens_block, tokens_block), 0)
    column = lax.broadcasted_iota(jnp.int32, (tokens_block, tokens_block), 1)
    before[...] = jnp.where(row < column, 1.0, 0.0).astype(bfloat)
    for copy in weights:
        copy.wait()
    first = (ctx * 4 + z) * local_exp

    def member(zz, p):
        yy = y + (p // 2) * (1 - 2 * y)
        cc = c + (p % 2) * (1 - 2 * c)
        return block_id(yy, cc, zz)

    def load_final(zz, p):
        return pltpu.make_async_copy(final_ref.at[member(zz, p)], pool.at[p], load_sem.at[p])

    def store_part(zz, p):
        return pltpu.make_async_copy(
            pool.at[4 + p % 2], part_ref.at[member(zz, p)], part_sem.at[p % 2]
        )

    def forward_group(step, carry):
        zz = line_order(z, step)
        after = step + 1 + inner * jnp.minimum(step, 1)

        @pl.when(after < 4)
        def _():
            forward(after)

        @pl.when(jnp.logical_and(step == 0, inner == 1))
        def _():
            forward(2)

        @pl.loop(0, 4)
        def _(p):
            load_final(zz, p).start()

        spread(CORE, block_id(y, 1 - c, zz)).wait_recv()
        spread(CORE, block_id(1 - y, c, zz)).wait_recv()
        spread(CORE, block_id(1 - y, c, zz)).start()
        spread(CORE, block_id(1 - y, 1 - c, zz)).wait_recv()

        @pl.loop(0, 4)
        def _(p):
            block = member(zz, p)
            tokens_in = held[block]
            logits = contract_last(router_ref[...], tokens_in)
            expert_row = lax.broadcasted_iota(jnp.int32, (experts, tokens_block), 0)
            routed = jnp.zeros((experts, tokens_block), single)
            for k in range(routes_ref.shape[1]):
                routed = routed + jnp.where(routes_ref[block, k : k + 1, :] == expert_row, 1.0, 0.0)
            named = routed > 0.5
            peak = jnp.max(jnp.where(named, logits, floor_score), axis=0, keepdims=True)
            raised = jnp.where(named, jnp.exp(jnp.minimum(logits - peak, 0.0)), 0.0)
            gates = raised / jnp.sum(raised, axis=0, keepdims=True)
            eight = lax.broadcasted_iota(jnp.int32, (8, tokens_block), 0)
            masks = jnp.zeros((8, tokens_block), single)
            own_mask = []
            own_gate = []
            for j in range(local_exp):
                here = expert_row == first + j
                own_mask.append(jnp.sum(jnp.where(here, routed, 0.0), axis=0, keepdims=True))
                own_gate.append(jnp.sum(jnp.where(here, gates, 0.0), axis=0, keepdims=True))
                masks = masks + jnp.where(eight == j, own_mask[j], 0.0)
            rank = matmul(masks.astype(bfloat), before[...])
            slot = lax.broadcasted_iota(jnp.int32, (capacity, tokens_block), 0).astype(single)
            for j in range(local_exp):
                hit = jnp.logical_and(slot == rank[j : j + 1, :], own_mask[j] > 0.5)
                pick = jnp.where(hit, 1.0, 0.0)
                picks[step * 4 + p, pl.ds(j * capacity, capacity), :] = pick.astype(bfloat)
                gate_column = jnp.sum(pick * own_gate[j], axis=1, keepdims=True)
                row_gates[p, pl.ds(j * capacity, capacity), :] = jnp.broadcast_to(
                    gate_column, (capacity, 128)
                )
            at = pl.multiple_of(step * group_rows + p * capacity, 32)
            for n in range(width // CHUNK):
                part = pl.ds(n * CHUNK, CHUNK)
                got = matmul(picks[step * 4 + p], held[block, :, part]).astype(bfloat)
                for j in range(local_exp):
                    rows_in[j, pl.ds(at, capacity), part] = got[j * capacity : (j + 1) * capacity]

        base = pl.multiple_of(step * group_rows, 128)
        for j in range(local_exp):
            given = rows_in[j, pl.ds(base, group_rows), :]
            for n in range(hidden_units // HALF):
                part = pl.ds(n * HALF, HALF)
                gate_pre = matmul(given, w_gate[j, :, part])
                up_pre = matmul(given, w_up[j, :, part])
                sigmoid = 1.0 / (1.0 + jnp.exp(-gate_pre))
                silu = gate_pre * sigmoid
                hidden_e[j, pl.ds(base, group_rows), part] = (silu * up_pre).astype(bfloat)
                slope_gate[j, pl.ds(base, group_rows), part] = (
                    up_pre * sigmoid * (1.0 + gate_pre * (1.0 - sigmoid))
                ).astype(bfloat)
                slope_up[j, pl.ds(base, group_rows), part] = silu.astype(bfloat)
            for n in range(width // CHUNK):
                part = pl.ds(n * CHUNK, CHUNK)
                work[j, :, part] = matmul(
                    hidden_e[j, pl.ds(base, group_rows), :], w_down[j, :, part]
                ).astype(bfloat)

        @pl.loop(0, 4)
        def _(p):
            block = member(zz, p)
            at = pl.multiple_of(step * group_rows + p * capacity, 32)
            local = pl.multiple_of(p * capacity, 32)
            pick = picks[step * 4 + p]
            weight = row_gates[p][:, 0:1]
            weighted = (pick.astype(single) * weight).astype(bfloat)
            load_final(zz, p).wait()

            @pl.when(jnp.logical_or(step > 0, p > 1))
            def _():
                store_part(zz, p).wait()

            row_score = jnp.zeros((local_exp * capacity, 1), single)
            for n in range(width // CHUNK):
                part = pl.ds(n * CHUNK, CHUNK)
                out = jnp.concatenate(
                    [work[j, pl.ds(local, capacity), part] for j in range(local_exp)], axis=0
                )
                pool[4 + p % 2, :, part] = contract_rows(weighted, out).astype(bfloat)
                final = matmul(pick, pool[p, :, part])
                row_score = row_score + jnp.sum(final * out.astype(single), axis=1, keepdims=True)
                graded = (final * weight).astype(bfloat)
                for j in range(local_exp):
                    rows_grad[j, pl.ds(at, capacity), part] = graded[j * capacity : (j + 1) * capacity]
            store_part(zz, p).start()
            spread_score = pick.astype(single) * row_score
            eight = lax.broadcasted_iota(jnp.int32, (8, tokens_block), 0)
            scores = jnp.zeros((8, tokens_block), single)
            for j in range(local_exp):
                total = jnp.sum(spread_score[j * capacity : (j + 1) * capacity], axis=0, keepdims=True)
                scores = scores + jnp.where(eight == j, total, 0.0)
            score_ref[block] = scores

        return carry

    lax.fori_loop(0, 4, forward_group, 0)

    def score_copy(block, source):
        return pltpu.make_async_remote_copy(
            src_ref=score_ref.at[block],
            dst_ref=score_got.at[source],
            send_sem=score_send.at[block],
            recv_sem=score_recv.at[source],
            device_id=member_device(block),
            device_id_type=MESH_ID,
        )

    @pl.loop(1, 16)
    def _(shift):
        score_copy((mine + shift) % 16, mine).start()

    score_got[mine] = score_ref[mine]

    @pl.loop(2, 4)
    def _(p):
        store_part(line_order(z, 3), p).wait()

    @pl.loop(0, 4)
    def _(zz):
        block = block_id(y, c, zz)
        for kind in (UP, DOWN):

            @pl.when(along(kind, zz))
            def _():
                spread(kind, block).wait_send()

        spread(ACROSS, block).wait_send()
        spread(CORE, block).wait_send()
        spread(CORE, block_id(1 - y, c, zz)).wait_send()

    opposite = {UP: DOWN, DOWN: UP, ACROSS: ACROSS, CORE: CORE}
    per_side(
        lambda kind: pl.semaphore_signal(
            ready.at[opposite[kind]], inc=1, device_id=device(kind), device_id_type=MESH_ID
        )
    )

    def sum_copy(kind, source, target, send_index, recv_sem):
        return pltpu.make_async_remote_copy(
            src_ref=source,
            dst_ref=target,
            send_sem=sum_send.at[send_index],
            recv_sem=recv_sem,
            device_id=device(kind),
            device_id_type=MESH_ID,
        )

    def to_core(turn, p, zz):
        slot = (y + p * (1 - 2 * y)) * 4 + zz
        index = turn * 2 + p
        return sum_copy(CORE, pool.at[index], held.at[slot], index, core_recv.at[slot])

    def from_core(slot):
        return sum_copy(CORE, pool.at[0], held.at[slot], 0, core_recv.at[slot])

    def to_across(zz):
        return sum_copy(ACROSS, held.at[(1 - y) * 4 + zz], held.at[8 + zz], 4 + zz, y_recv.at[zz])

    def to_line(kind, zz, last):
        return sum_copy(
            kind,
            held.at[y * 4 + zz],
            pool.at[5] if last else held.at[12 + zz],
            8 + zz,
            z_recv.at[4 if last else zz],
        )

    def add_up(slot, *others):
        @pl.loop(0, tokens_block // 64)
        def _(r):
            rows = pl.ds(pl.multiple_of(r * 64, 64), 64)
            total = held[slot, rows, :].astype(single)
            for ref, index in others:
                total = total + ref[index, rows, :].astype(single)
            held[slot, rows, :] = total.astype(bfloat)

    def back_block(step, p, target, index, onto):
        local = pl.multiple_of(p * capacity, 32)
        pick = picks[step * 4 + p]
        for n in range(width // CHUNK):
            part = pl.ds(n * CHUNK, CHUNK)
            grads = jnp.concatenate(
                [work[j, pl.ds(local, capacity), part] for j in range(local_exp)], axis=0
            )
            block = contract_rows(pick, grads)
            if onto:
                block = block + target[index, :, part].astype(single)
            target[index, :, part] = block.astype(bfloat)

    def line_sum(step):
        zz = line_order(z, step)
        slot = y * 4 + zz
        to_across(zz).wait_recv()
        rising = zz > z
        comes = jnp.logical_or(jnp.logical_and(rising, z > 0), jnp.logical_and(zz < z, z < 3))

        @pl.when(comes)
        def _():
            to_line(CORE, zz, False).wait_recv()
            add_up(slot, (held, 8 + zz), (held, 12 + zz))

        @pl.when(jnp.logical_not(comes))
        def _():
            add_up(slot, (held, 8 + zz))

        @pl.when(rising)
        def _():
            to_line(UP, zz, False).start()

        @pl.when(zz == z - 1)
        def _():
            to_line(DOWN, zz, True).start()

        @pl.when(zz < z - 1)
        def _():
            to_line(DOWN, zz, False).start()

    def at_end(action):
        pl.when(inner == 0)(action)

    def at_middle(action):
        pl.when(inner == 1)(action)

    def backward_group(turn_step, carry):
        step = 3 - turn_step
        zz = line_order(z, step)
        turn = step % 2
        base = pl.multiple_of(step * group_rows, 128)
        for j in range(local_exp):
            for n in range(hidden_units // HALF):
                part = pl.ds(n * HALF, HALF)
                grad_hidden = (
                    contract_last(rows_grad[j, pl.ds(base, group_rows), :], w_down[j, part, :])
                    .astype(bfloat)
                    .astype(single)
                )
                slope_gate[j, pl.ds(base, group_rows), part] = (
                    grad_hidden * slope_gate[j, pl.ds(base, group_rows), part].astype(single)
                ).astype(bfloat)
                slope_up[j, pl.ds(base, group_rows), part] = (
                    grad_hidden * slope_up[j, pl.ds(base, group_rows), part].astype(single)
                ).astype(bfloat)
            for n in range(width // CHUNK):
                part = pl.ds(n * CHUNK, CHUNK)
                work[j, :, part] = (
                    contract_last(slope_gate[j, pl.ds(base, group_rows), :], w_gate[j, part, :])
                    + contract_last(slope_up[j, pl.ds(base, group_rows), :], w_up[j, part, :])
                ).astype(bfloat)

        @pl.when(turn_step == 0)
        def _():
            per_side(lambda kind: pl.semaphore_wait(ready.at[kind], 1))

        for p, member_p in ((1, 3), (0, 1)):

            @pl.when(turn_step > 1)
            def _():
                to_core(turn, p, zz).wait_send()

            back_block(step, member_p, pool, turn * 2 + p, False)
            to_core(turn, p, zz).start()

        other = (1 - y) * 4 + zz
        from_core(other).wait_recv()
        back_block(step, 2, held, other, True)
        to_across(zz).start()
        slot = y * 4 + zz
        from_core(slot).wait_recv()
        back_block(step, 0, held, slot, True)

        @pl.when(turn_step == 2)
        def _():
            at_end(lambda: line_sum(3))

        return carry

    lax.fori_loop(0, 4, backward_group, 0)
    at_middle(lambda: line_sum(3))
    at_end(lambda: line_sum(2))

    def stores(j):
        pairs = ((w_gate, grad_gate_ref), (w_up, grad_up_ref), (w_down, grad_down_ref))
        if not swap:
            return [
                pltpu.make_async_copy(source.at[j], target.at[j], load_sem.at[3 * j + i])
                for i, (source, target) in enumerate(pairs)
            ]
        d = lax.axis_index("dp")
        copies = []
        for i, (source, target) in enumerate(pairs):
            size = target.shape[1]
            here = pl.ds(pl.multiple_of(d * size, 128), size)
            copies.append(
                pltpu.make_async_copy(source.at[j, here, :], target.at[j], load_sem.at[3 * j + i])
            )
        there = lambda size: pl.ds(pl.multiple_of((1 - d) * size, 128), size)
        low = w_down.shape[1] // 2
        leaving = [
            (
                w_down.at[j, there(low), pl.ds(n * hidden_units, hidden_units)],
                swap[2].at[2 + j, pl.ds(n * low, low), :],
            )
            for n in range(width // hidden_units)
        ]
        if j == 1:
            leaving += [
                (source.at[1, there(width // 2), :], swap[2].at[i])
                for i, source in enumerate((w_gate, w_up))
            ]
        for i, (source, target) in enumerate(leaving):
            copies.append(pltpu.make_async_copy(source, target, load_sem.at[6 + 3 * j + i]))
        return copies

    def weight_grads(j):
        @pl.loop(0, width // CHUNK)
        def _(n):
            part = pl.ds(pl.multiple_of(n * CHUNK, CHUNK), CHUNK)
            w_gate[j, part, :] = contract_rows(rows_in[j, :, part], slope_gate[j]).astype(bfloat)
            w_up[j, part, :] = contract_rows(rows_in[j, :, part], slope_up[j]).astype(bfloat)
            w_down[j, :, part] = contract_rows(hidden_e[j], rows_grad[j, :, part]).astype(bfloat)

        for copy in stores(j):
            copy.start()

    weight_grads(0)
    swaps = []
    if swap:
        swaps = swap_copies(
            ((w_gate, 0, swap[0]), (w_up, 0, swap[1])), device, swap_send, swap_recv
        )
        for copy in swaps:
            copy.start()
    weight_grads(1)
    at_middle(lambda: line_sum(2))
    line_sum(1)
    slot = y * 4 + z
    to_across(z).wait_recv()
    add_up(slot, (held, 8 + z))

    @pl.when(z > 0)
    def _():
        to_line(CORE, z, False).wait_recv()
        add_up(slot, (held, 12 + z))

    @pl.when(z < 3)
    def _():
        to_line(CORE, z, True).wait_recv()
        add_up(slot, (pool, 5))

    result = pltpu.make_async_copy(held.at[slot], back_ref, local_sem)
    result.start()
    for j in range(local_exp):
        for copy in stores(j):
            copy.wait()
    for turn in range(2):
        for p in range(2):
            to_core(turn, p, z).wait_send()

    @pl.loop(0, 4)
    def _(zz):
        to_across(zz).wait_send()

        @pl.when(zz != z)
        def _():
            to_line(CORE, zz, False).wait_send()

    @pl.loop(1, 16)
    def _(shift):
        other = (mine + shift) % 16
        score_copy(other, mine).wait_send()
        score_copy(other, other).wait_recv()

    for copy in swaps:
        copy.wait()
    result.wait()


def experts_on_owner(
    hidden, final_all, routes_all, router_rows, w_gate, w_up, w_down, capacity, swap
):
    blocks = final_all.shape[0]
    tokens_block, width = hidden.shape
    local_exp, _, units = w_gate.shape
    bfloat = jnp.bfloat16
    single = jnp.float32
    rows = blocks * capacity
    grads = [x.shape for x in (w_gate, w_up, w_down)]
    if swap:
        wide, low = (width // 2, units), (units // 2, width)
        grads = [(2, *wide), (2, *wide), (2, *low), wide, wide, (4, *wide)]
    anywhere = pl.BlockSpec(memory_space=pl.ANY)
    vmem = pl.BlockSpec(memory_space=pltpu.VMEM)
    dma = pltpu.SemaphoreType.DMA
    return pl.pallas_call(
        functools.partial(experts_kernel, swap),
        out_shape=(
            jax.ShapeDtypeStruct((tokens_block, width), bfloat),
            jax.ShapeDtypeStruct((blocks, tokens_block, width), bfloat),
            jax.ShapeDtypeStruct((blocks, 8, tokens_block), single),
            *(jax.ShapeDtypeStruct(shape, bfloat) for shape in grads),
        ),
        in_specs=[anywhere, anywhere, vmem, vmem, anywhere, anywhere, anywhere],
        out_specs=(anywhere, anywhere, vmem, *([anywhere] * len(grads))),
        scratch_shapes=[
            pltpu.VMEM((blocks, tokens_block, width), bfloat),
            pltpu.VMEM(w_gate.shape, bfloat),
            pltpu.VMEM(w_up.shape, bfloat),
            pltpu.VMEM(w_down.shape, bfloat),
            pltpu.VMEM((local_exp, rows, width), bfloat),
            pltpu.VMEM((local_exp, rows, width), bfloat),
            pltpu.VMEM((local_exp, rows, units), bfloat),
            pltpu.VMEM((local_exp, rows, units), bfloat),
            pltpu.VMEM((local_exp, rows, units), bfloat),
            pltpu.VMEM((blocks, local_exp * capacity, tokens_block), bfloat),
            pltpu.VMEM((4, local_exp * capacity, 128), single),
            pltpu.VMEM((local_exp, 4 * capacity, width), bfloat),
            pltpu.VMEM((6, tokens_block, width), bfloat),
            pltpu.VMEM((tokens_block, tokens_block), bfloat),
            dma((4, blocks)),
            dma((blocks,)),
            dma,
            dma((14,)),
            dma((2,)),
            dma((12,)),
            dma((8,)),
            dma((4,)),
            dma((5,)),
            pltpu.SemaphoreType.REGULAR((4,)),
            pltpu.VMEM((blocks, 8, tokens_block), single),
            dma((16,)),
            dma((16,)),
            dma((2,)),
            dma((2,)),
        ],
        compiler_params=pltpu.CompilerParams(
            collective_id=1, has_side_effects=True, vmem_limit_bytes=63 * 2**20
        ),
        name="experts",
    )(hidden, final_all, routes_all, router_rows, w_gate, w_up, w_down)


def on_device(
    tokens,
    lengths,
    routes,
    gain_attn,
    w_query,
    key_weight,
    value_weight,
    w_out,
    gain_ffn,
    w_router,
    w_gate,
    w_up,
    w_down,
    cotangent,
):
    tokens_own = tokens.shape[1]
    exp_count = lax.axis_size("expert")
    ctx_count = lax.axis_size("context")
    local_exp = w_gate.shape[0]
    experts = local_exp * ctx_count * exp_count
    capacity = tokens_own * TOP * 3 // (2 * experts)
    bfloat = jnp.bfloat16
    single = jnp.float32
    query_width = w_query.shape[1]
    key_width = key_weight.shape[1]
    proj_width = query_width + 2 * key_width
    own_rows = w_query.shape[0]
    pair = lax.axis_size("dp") == 2
    small = jnp.concatenate(
        [
            w_router,
            gain_attn[:, None],
            gain_ffn[:, None],
            jnp.zeros((own_rows, 64 - experts - 2), bfloat),
        ],
        axis=1,
    )
    if pair:
        packed = routes[0].T.reshape(-1, 64).astype(bfloat)
        packed = jnp.pad(packed, ((0, own_rows - packed.shape[0]), (0, 0)))
        early, small_all, out_w = gather_weights(
            w_query, key_weight, value_weight, jnp.concatenate([small, packed], axis=1), w_out
        )
        out_w = out_w.reshape(-1, out_w.shape[2])
        routes_all = lax.dynamic_slice(
            small_all, (lax.axis_index("dp") * 16, 0, 64), (16, tokens_own * TOP // 64, 64)
        )
        routes_all = routes_all.astype(jnp.int32).reshape(16, TOP, tokens_own)
        proj_w = early.reshape(-1, proj_width)
        small_all = small_all.reshape(-1, small_all.shape[2])
    else:
        proj_w = jnp.concatenate([w_query, key_weight, value_weight], axis=1)
        proj_w = lax.all_gather(proj_w, EVERY, axis=0, tiled=True)
        small_all = lax.all_gather(small, EVERY, axis=0, tiled=True)
        out_w = lax.all_gather(w_out, EVERY, axis=0, tiled=True)
        routes_all = lax.all_gather(routes[0].T, GROUP, axis=0, tiled=False)
    positions = lax.axis_index("context") * tokens_own + jnp.arange(tokens_own, dtype=jnp.int32)
    valid = (positions < lengths[0]).astype(single)[:, None]
    grad_final = cotangent[0].astype(single) * valid
    final_all = lax.all_gather(grad_final.astype(bfloat), GROUP, axis=0, tiled=False)
    router_w = small_all[:, :experts]
    gain_one = small_all[:, experts].astype(single)
    gain_two = small_all[:, experts + 1].astype(single)
    cosine, sine = rotation_tables(positions)

    inputs = tokens[0].astype(single)
    inverse_one = lax.rsqrt(jnp.mean(inputs * inputs, axis=-1, keepdims=True) + epsilon)
    normed_one = inputs * inverse_one
    hidden_one = lax.optimization_barrier((normed_one * gain_one).astype(bfloat))
    projected = jnp.einsum("de,sd->es", proj_w, hidden_one, preferred_element_type=single)
    rotated = apply_rotation(projected[: query_width + key_width], cosine, sine).astype(bfloat)
    query = rotated[:query_width] * HEAD_SIZE ** (-0.5)
    own_pairs = jnp.concatenate(
        [rotated[query_width:], projected[query_width + key_width :].astype(bfloat)], axis=0
    )
    mixed, pairs = attend(query, own_pairs, lengths)
    resid = inputs + jnp.einsum("es,ed->sd", mixed, out_w, preferred_element_type=single)
    inverse_two = lax.rsqrt(jnp.mean(resid * resid, axis=-1, keepdims=True) + epsilon)
    normed_two = resid * inverse_two
    hidden_two = (normed_two * gain_two).astype(bfloat)

    grad_hidden, combined, scores, *expert_grads = experts_on_owner(
        hidden_two, final_all, routes_all, router_w.T, w_gate, w_up, w_down, capacity, pair
    )
    expert_grads, got = expert_grads[:3], expert_grads[3:]
    combined = lax.psum_scatter(combined, GROUP, scatter_dimension=0, tiled=False)

    if pair:
        moved = lax.ppermute(got[2], "dp", ((0, 1), (1, 0)))
        low = w_down.shape[1] // 2
        others = (
            jnp.stack([got[0], moved[0]]),
            jnp.stack([got[1], moved[1]]),
            jnp.concatenate(
                [moved[2:, n * low : (n + 1) * low] for n in range(MODEL_WIDTH // w_down.shape[1])],
                axis=2,
            ),
        )
    scores = scores[:, :local_exp]
    grad_gates = scores.reshape(experts, tokens_own).T

    routed = jnp.any(routes[0][:, :, None] == jnp.arange(experts, dtype=jnp.int32), axis=1)
    logits = jnp.einsum("sd,de->se", hidden_two, router_w, preferred_element_type=single)
    gates = jax.nn.softmax(jnp.where(routed, logits, floor_score), axis=-1)
    gates = jnp.where(routed, gates, 0.0)
    gate_mean = jnp.sum(gates * grad_gates, axis=-1, keepdims=True)
    grad_logits = (gates * (grad_gates - gate_mean)).astype(bfloat)
    grad_w_router = jnp.einsum("sd,se->de", hidden_two, grad_logits, preferred_element_type=single)
    grad_hidden_two = grad_hidden.astype(single) + jnp.einsum(
        "se,de->sd", grad_logits, router_w, preferred_element_type=single
    )
    grad_gain_ffn = jnp.sum(grad_hidden_two * normed_two, axis=0)
    grad_resid = norm_back(grad_hidden_two * gain_two, normed_two, inverse_two) + grad_final
    grad_attn = lax.optimization_barrier(grad_resid.astype(bfloat))

    grad_out_w = jnp.einsum("es,sd->ed", mixed, grad_attn, preferred_element_type=single)
    grad_mixed = jnp.einsum("ed,sd->es", out_w, grad_attn, preferred_element_type=single)
    grad_out_w = grad_out_w.astype(bfloat)
    grad_proj = attend_back(query, pairs, grad_mixed.astype(bfloat), lengths, cosine, sine)
    grad_proj_w = jnp.einsum("sd,es->de", hidden_one, grad_proj, preferred_element_type=single)
    grad_hidden_one = jnp.einsum("es,de->sd", grad_proj, proj_w, preferred_element_type=single)
    grad_gain_attn = jnp.sum(grad_hidden_one * normed_one, axis=0)
    grad_tokens = norm_back(grad_hidden_one * gain_one, normed_one, inverse_one) + grad_resid

    grad_small = jnp.concatenate(
        [
            grad_w_router,
            grad_gain_attn[:, None],
            grad_gain_ffn[:, None],
            jnp.zeros((MODEL_WIDTH, 128 - experts - 2), single),
        ],
        axis=1,
    ).astype(bfloat)
    grad_proj_w = grad_proj_w.astype(bfloat)
    if pair:
        expert_sums = tuple(
            own.astype(single) + other.astype(single)
            for own, other in zip(expert_grads, others)
        )
        grad_proj_w, grad_tokens, expert_sums = lax.optimization_barrier(
            (grad_proj_w, grad_tokens, expert_sums)
        )
        *proj_sums, small_sum, out_sum = sum_gradients(
            grad_proj_w, grad_small, grad_out_w, (query_width, key_width, key_width)
        )
    else:
        summed = lax.psum_scatter(
            jnp.concatenate([grad_proj_w, grad_small, grad_out_w], axis=1),
            EVERY,
            scatter_dimension=0,
            tiled=True,
        ).astype(single)
        proj_sums = jnp.split(summed[:, :proj_width], (query_width, query_width + key_width), axis=1)
        small_sum = summed[:, proj_width : proj_width + 128]
        out_sum = summed[:, proj_width + 128 :]
        expert_sums = tuple(
            lax.psum_scatter(x, "dp", scatter_dimension=1, tiled=True).astype(single)
            for x in expert_grads
        )
    combined, small_sum = lax.optimization_barrier((combined, small_sum))
    block_out = (valid * (resid + combined.astype(single))).astype(bfloat)
    return (
        block_out[None],
        grad_tokens[None],
        small_sum[:, experts],
        *proj_sums,
        out_sum,
        small_sum[:, experts + 1],
        small_sum[:, :experts],
        *expert_sums,
    )


def solution(mesh):
    in_specs = (
        P(("dp", "expert"), "context", None),
        P(("dp", "expert")),
        P(("dp", "expert"), "context", None),
        P(("dp", "context", "expert")),
        P(("dp", "context", "expert"), None),
        P(("dp", "context", "expert"), None),
        P(("dp", "context", "expert"), None),
        P(("dp", "context", "expert"), None),
        P(("dp", "context", "expert")),
        P(("dp", "context", "expert"), None),
        P(("context", "expert"), None, None),
        P(("context", "expert"), None, None),
        P(("context", "expert"), None, None),
        P(("dp", "expert"), "context", None),
    )
    out_specs = (
        P(("dp", "expert"), "context", None),
        P(("dp", "expert"), "context", None),
        P(("dp", "context", "expert")),
        P(("dp", "context", "expert"), None),
        P(("dp", "context", "expert"), None),
        P(("dp", "context", "expert"), None),
        P(("dp", "context", "expert"), None),
        P(("dp", "context", "expert")),
        P(("dp", "context", "expert"), None),
        P(("context", "expert"), "dp", None),
        P(("context", "expert"), "dp", None),
        P(("context", "expert"), "dp", None),
    )
    return jax.shard_map(
        on_device, mesh=mesh, in_specs=in_specs, out_specs=out_specs, check_vma=False
    )
```

profile of v0, /device:TPU:0, one launch (start us, length us, event | category | flops | bytes accessed | tf_op | source)
XLA Modules:
  0.0 514.9 jit_solution(11885194020783479402)
XLA Ops:
  7.9 2.3 fusion.4
  10.7 0.7 concatenate.20.small_ref
  11.4 95.8 %gather_weights.1 = (bf16[32,48,2560]{2,1,0:T(8,128)(2,1)}, bf16[32,48,128]{2,1,0:T(8,128)(2,1)}, bf16[32,48,1536]{2,1,0:T(8,128)(2,1)}) custom-call(bf16[48,1536]{1,0:T(8,128)(2,1)} %query_ref.1, bf16[48,512]{1,0:T(8,128)(2,1)} %key_ref.1, bf16[48,512]{1,0:T(8,128)(2,1)} %value_ref.1, bf16[48,128]{1,0:T(8,128)(2,1)} %concatenate.20.small_ref, ...), custom_call_target="tpu_custom_call" | custom-call | tf_op jit(solution)/shard_map/gather_weights/pallas_call | solution.py:434
  107.3 1.7 convert_reduce_fusion
  109.0 0.2 fusion.13
  109.2 0.3 fusion.7
  109.5 6.6 %fusion.30 = f32[2560,256]{1,0:T(8,128)S(1)} fusion(bf16[1536,2560]{1,0:T(8,128)(2,1)} %bitcast.90, bf16[256,1536]{1,0:T(8,128)(2,1)S(1)} %fusion.7), kind=kOutput, calls=%fused_computation.76 | convolution fusion | flops 2013265920 | bytes 11272192 | tf_op jit(solution)/shard_map/de,sd->es/dot_general | solution.py:1709
  116.2 1.5 slice.79
  117.8 0.8 reshape.206.routes_ref
  118.6 0.8 copy.68
  119.6 2.0 add_convert_fusion
  121.8 26.0 %attend.1 = (bf16[1536,256]{1,0:T(8,128)(2,1)S(1)}, bf16[4,1024,256]{2,1,0:T(8,128)(2,1)S(1)}) custom-call(bf16[1536,256]{1,0:T(8,128)(2,1)S(1)} %bitcast.66, bf16[1024,256]{1,0:T(8,128)(2,1)S(1)} %pad_maximum_fusion.own_ref, s32[1]{0:T(128)} %copy.73.length_ref), custom_call_target="tpu_custom_call" | custom-call | tf_op jit(solution)/shard_map/attend/pallas_call | solution.py:794
  147.8 1.5 multiply_reduce_fusion.2
  149.4 1.1 copy-done.5
  150.5 1.1 multiply_convert_fusion.1.hidden_ref
  151.6 176.3 %experts.1 = (bf16[256,1536]{1,0:T(8,128)(2,1)}, bf16[16,256,1536]{2,1,0:T(8,128)(2,1)}, f32[16,8,256]{2,1,0:T(8,128)}, bf16[2,768,512]{2,1,0:T(8,128)(2,1)}, bf...) custom-call(bf16[256,1536]{1,0:T(8,128)(2,1)} %multiply_convert_fusi, ...), custom_call_target="tpu_custom_call" | custom-call | tf_op jit(solution)/shard_map/experts/pallas_call | solution.py:1591
  328.0 1.0 copy-done.8
  329.0 1.4 fusion.29
  330.4 0.9 slice.69
  331.4 2.0 multiply_reduce_fusion
  333.5 1.7 fusion.25
  335.2 1.6 collective-permute-start
  336.8 5.4 %convolution_convert_fusion.2.grad_ref = bf16[1536,256]{1,0:T(8,128)(2,1)} fusion(bf16[1536,1536]{1,0:T(8,128)(2,1)} %bitcast.70, bf16[256,1536]{1,0:T(8,128)(2,1)S(1)} %get-tuple-element.132), kind=kOutput, calls=%fused_computation.7 | convolution fusion | flops 1208352768 | bytes 6291456 | tf_op jit(solution)/shard_map/ed,sd->es/dot_general | solution.py:1756
  342.2 0.7 concatenate.28
  342.9 1.9 copy-done.3
  344.8 1.3 copy-done.4
  346.0 41.0 %attend_back.1 = bf16[2560,256]{1,0:T(8,128)(2,1)S(1)} custom-call(bf16[1536,256]{1,0:T(8,128)(2,1)S(1)} %bitcast.67, bf16[4,1024,256]{2,1,0:T(8,128)(2,1)S(1)} %copy-done.3, bf16[1536,256]{1,0:T(8,128)(2,1)S(1)} %copy-done.4, s32[1]{0:T(128)} %copy.73.length_ref, f32[32,256]{1,0:T(8,128)S(1)} %get-tuple-element.141.cosine_ref, ...), custom_call_target="tpu_custom_call" | custom-call | flops 1048576 | bytes 65536 | tf_op jit(solution)/shard_map/attend_back/pallas_call | solution.py:975
  387.1 6.9 %fusion.12 = (bf16[1536]{0:T(1024)(128)(2,1)S(1)}, f32[256]{0:T(256)S(1)}, f32[256,1536]{1,0:T(8,128)}) fusion(bf16[1,256,1536]{2,1,0:T(8,128)(2,1)S(1)} %copy-done.11, f32[256]{0:T(256)S(1)} %add_rsqrt_fusion.1, f32[1536]{0:T(1024)S(1)} %get-tuple-element.129, bf16[2560,256]{1,0:T(8,128)(2,1)S(1)} %attend_back.1, bf16[1536,2560]{1,0:T(8,128)(2,1)} %bitcast.91), kind=kOutput, calls=%fused_computation.25 | convolution fusion | flops 2016016640 | bytes 11545600 | tf_op jit(solution)/shard_map/es,de->sd/dot_general | solution.py:1760
  394.0 1.5 concatenate.27
  395.7 0.2 copy.64
  396.0 2.2 maximum_maximum_fusion.small_ref
  398.2 3.6 convolution_convert_fusion.1
  401.8 5.4 %convolution_convert_fusion = bf16[1536,2560]{1,0:T(8,128)(2,1)} fusion(bf16[256,1536]{1,0:T(8,128)(2,1)S(1)} %copy-done.16, bf16[2560,256]{1,0:T(8,128)(2,1)S(1)} %attend_back.1), kind=kOutput, calls=%fused_computation | convolution fusion | flops 2017198080 | bytes 9961472 | tf_op jit(solution)/shard_map/sd,es->de/dot_general | solution.py:1759
  407.2 1.6 fusion.11
  408.7 1.8 fusion.27
  410.5 1.6 fusion.28
  412.2 0.3 copy-done.20
  412.5 0.5 copy-done.21
  412.9 3.7 convert_add_fusion.1
  416.7 2.1 convert_add_fusion
  418.8 82.3 %sum_gradients.1 = (f32[48,1536]{1,0:T(8,128)}, f32[48,512]{1,0:T(8,128)}, f32[48,512]{1,0:T(8,128)}, f32[48,128]{1,0:T(8,128)}, f32[48,1536]{1,0:T(8,128)}) custom-call(bf16[2,16,48,2560]{3,2,1,0:T(8,128)(2,1)} %bitcast.68, bf16[2,16,48,128]{3,2,1,0:T(8,128)(2,1)} %maximum_maximum_fusion.small_ref, bf16[2,16,48,1536]{3,2,1,0:T(8,128)(2,1)} %bitcast.69), custom_call_target="tpu_custom_call" | custom-call | flops 1048576 | bytes 65536 | tf_op jit(solution)/shard_map/sum_gradients/pallas_call | solution.py:644
  501.2 2.3 fusion.16
  503.5 0.7 slice_reduce_fusion
  504.2 0.7 copy.67
  504.9 0.7 copy.74
  505.6 0.6 copy.75
  506.2 0.6 copy.76
  506.9 0.7 copy.77
  (104 shorter events, 1.7 us)
Async XLA Ops:
  7.2 3.1 copy-start.32
  7.2 3.2 copy-start.33
  7.2 3.3 copy-start.34
  7.2 3.4 copy-start.31
  7.2 144.4 %all-gather.2.cloned.1.call-start = ((), (), s32[]{:S(2)}) async-start(), calls=%async_computation.1 | async-start | bytes 13369344 | tf_op jit(solution)/shard_map/all_gather | solution.py:1699
  7.9 101.0 %copy-start.10 = (bf16[1,256,1536]{2,1,0:T(8,128)(2,1)S(1)}, bf16[1,256,1536]{2,1,0:T(8,128)(2,1)}, u32[]{:S(2)}) copy-start(bf16[1,256,1536]{2,1,0:T(8,128)(2,1)} %param.14) | copy-start | bytes 2359300
  10.2 490.9 %reduce-scatter.2.cloned.1.call-start = ((), (), s32[]{:S(2)}) async-start(), calls=%async_computation.2 | async-start | bytes 13369344 | tf_op jit(solution)/shard_map/reduce_scatter | solution.py:1725
  109.5 6.7 %copy-start.15 = (bf16[256,1536]{1,0:T(8,128)(2,1)}, bf16[256,1536]{1,0:T(8,128)(2,1)S(1)}, u32[]{:S(2)}) copy-start(bf16[256,1536]{1,0:T(8,128)(2,1)S(1)} %fusion.7) | copy-start | bytes 2359300
  116.1 1.5 copy-start.13
  116.1 31.7 %slice-start = ((s8[4718592]{0:T(1024)(128)(4,1)}), s8[524288]{0:T(1024)(128)(4,1)S(1)}, s32[]{:S(2)}) async-start(s8[4718592]{0:T(1024)(128)(4,1)} %bitcast.71), calls=%async_computation.3 | async-start | bytes 1048576
  119.6 28.2 %slice-start.1 = ((s8[4718592]{0:T(1024)(128)(4,1)}), s8[4194304]{0:T(1024)(128)(4,1)S(1)}, s32[]{:S(2)}) async-start(s8[4718592]{0:T(1024)(128)(4,1)} %bitcast.71), calls=%async_computation.4 | async-start | bytes 8388608
  121.8 27.5 %copy-start = (bf16[24,2,32,256]{3,2,1,0:T(8,128)(2,1)}, bf16[24,2,32,256]{3,2,1,0:T(8,128)(2,1)S(1)}, u32[]{:S(2)}) copy-start(bf16[24,2,32,256]{3,2,1,0:T(8,128)(2,1)S(1)} %fusion.15) | copy-start | bytes 2359300
  147.8 1.5 copy-start.2
  149.3 1.2 copy-start.5
  327.9 1.1 copy-start.8
  327.9 3.5 copy-start.6
  331.4 2.1 copy-start.19
  335.2 7.0 %copy-start.17 = (bf16[256,1536]{1,0:T(8,128)(2,1)}, bf16[256,1536]{1,0:T(8,128)(2,1)S(1)}, u32[]{:S(2)}) copy-start(bf16[256,1536]{1,0:T(8,128)(2,1)S(1)} %get-tuple-element.132) | copy-start | bytes 2359300
  335.2 7.7 %copy-start.1 = (bf16[24,2,32,256]{3,2,1,0:T(8,128)(2,1)S(1)}, bf16[24,2,32,256]{3,2,1,0:T(8,128)(2,1)}, u32[]{:S(2)}) copy-start(bf16[24,2,32,256]{3,2,1,0:T(8,128)(2,1)} %copy-done) | copy-start | bytes 2359300
  335.2 73.6 %collective-permute-start = (bf16[4,768,512]{2,1,0:T(8,128)(2,1)}, bf16[4,768,512]{2,1,0:T(8,128)(2,1)}, u32[]{:S(2)}, u32[]{:S(2)}) collective-permute-start(bf16[4,768,512]{2,1,0:T(8,128)(2,1)} %get-tuple-element.48), channel_id=1, source_target_pairs={{0,16},{16,0},{1,17},{17,1},{2,18},{18,2},{3,19},{19,3},{4,20},{20... | collective-permute-start | bytes 9437192 | tf_op jit(solution)/shard_map/ppermute | solution.py:1728
  342.9 1.9 copy-start.3
  344.8 1.3 copy-start.4
  346.0 41.0 %copy-start.11 = (bf16[1,256,1536]{2,1,0:T(8,128)(2,1)S(1)}, bf16[1,256,1536]{2,1,0:T(8,128)(2,1)}, u32[]{:S(2)}) copy-start(bf16[1,256,1536]{2,1,0:T(8,128)(2,1)} %param.14) | copy-start | bytes 2359300
  387.1 8.4 %copy-start.9 = (bf16[256,1536]{1,0:T(8,128)(2,1)S(1)}, bf16[256,1536]{1,0:T(8,128)(2,1)}, u32[]{:S(2)}) copy-start(bf16[256,1536]{1,0:T(8,128)(2,1)} %multiply_convert_fusion.1.hidden_ref) | copy-start | bytes 2359300
  395.9 2.2 copy-start.18
  398.2 3.6 copy-start.16
  401.8 5.4 %copy-start.12 = (bf16[1,256,1536]{2,1,0:T(8,128)(2,1)S(1)}, bf16[1,256,1536]{2,1,0:T(8,128)(2,1)}, u32[]{:S(2)}) copy-start(bf16[1,256,1536]{2,1,0:T(8,128)(2,1)} %param.14) | copy-start | bytes 2359300
  401.8 5.4 %copy-start.14 = (f32[256,1536]{1,0:T(8,128)S(1)}, f32[256,1536]{1,0:T(8,128)}, u32[]{:S(2)}) copy-start(f32[256,1536]{1,0:T(8,128)} %get-tuple-element.133) | copy-start | bytes 4718596
  401.8 5.4 %copy-start.23 = (f32[256,1536]{1,0:T(8,128)S(1)}, f32[256,1536]{1,0:T(8,128)}, u32[]{:S(2)}) copy-start(f32[256,1536]{1,0:T(8,128)} %get-tuple-element.148) | copy-start | bytes 4718596
  408.7 3.4 copy-start.24
  408.7 3.4 copy-start.25
  410.5 1.9 copy-start.20
  410.5 2.4 copy-start.21
  412.9 3.7 copy-start.22
  418.8 82.3 %copy-start.7 = (f32[256,1536]{1,0:T(8,128)S(1)}, f32[256,1536]{1,0:T(8,128)}, u32[]{:S(2)}) copy-start(f32[256,1536]{1,0:T(8,128)} %copy-done.5) | copy-start | bytes 4718596
  501.1 2.4 copy-start.28
  501.1 3.7 copy-start.27
  501.1 4.4 copy-start.30
  501.2 5.1 copy-start.29
  501.2 5.7 %copy-start.26 = (f32[48,1536]{1,0:T(8,128)S(1)}, f32[48,1536]{1,0:T(8,128)}, u32[]{:S(2)}) copy-start(f32[48,1536]{1,0:T(8,128)} %get-tuple-element.169) | copy-start | bytes 884740
Sparse Core Ops, SparseCore 0:
  10.9 116.3 all-gather.1
  328.0 145.1 reduce-scatter.1
where the time goes:
time: 522 us; the launch traced here: 515 us
  Pallas kernels  421 us (81%)
  matrix products  33 us (6%)
  other arithmetic  21.8 us (4%)
  local copies, waits for them, and re-layouts  21.2 us (4%)
  between operations  15.7 us (3%)
    pallas_call x1, Pallas kernels, experts_on_owner(): pl.pallas_call(functools.partial(experts_kernel, swap), out_shape=(jax.Sh...  176 us
    pallas_call x1, Pallas kernels, gather_weights(): pl.pallas_call(gather_kernel, out_shape=tuple((jax.ShapeDtypeStruct((32,...  95.8 us
    pallas_call x1, Pallas kernels, sum_gradients(): pl.pallas_call(sums_kernel, out_shape=(*(jax.ShapeDtypeStruct((rows, size...  82.3 us
    pallas_call x1, Pallas kernels, attend_back(): pl.pallas_call(attend_back_kernel, out_shape=jax.ShapeDtypeStruct((query....  41 us
    pallas_call x1, Pallas kernels, attend(): pl.pallas_call(attend_kernel, out_shape=(jax.ShapeDtypeStruct(query.shape...  26 us
  transfers between devices with their start and end apart: 3, of which 0 were waited for; matrix products, arithmetic and copies ran while one was open for 12% of the time, Pallas kernels for 48%

commit v1 on v0

--- a/solution.py
+++ b/solution.py
@@ -612,6 +612,9 @@
     @pl.loop(0, 4)
     def _(turn):
         meet(3 - turn)
+
+    @pl.loop(0, 4)
+    def _(turn):
         out_across(3 - turn)
 
     @pl.loop(0, 4)

time: 522 us -> 522 us (level)
  no operation moved by 1% of the time
where the time goes in v1:
time: 522 us; the launch traced here: 515 us
  Pallas kernels  421 us (81%)
  matrix products  33 us (6%)
  other arithmetic  21.8 us (4%)
  local copies, waits for them, and re-layouts  21.2 us (4%)
  between operations  15.7 us (3%)
    pallas_call x1, Pallas kernels, experts_on_owner(): pl.pallas_call(functools.partial(experts_kernel, swap), out_shape=(jax.Sh...  176 us
    pallas_call x1, Pallas kernels, gather_weights(): pl.pallas_call(gather_kernel, out_shape=tuple((jax.ShapeDtypeStruct((32,...  95.8 us
    pallas_call x1, Pallas kernels, sum_gradients(): pl.pallas_call(sums_kernel, out_shape=(*(jax.ShapeDtypeStruct((rows, size...  82.3 us
    pallas_call x1, Pallas kernels, attend_back(): pl.pallas_call(attend_back_kernel, out_shape=jax.ShapeDtypeStruct((query....  41 us
    pallas_call x1, Pallas kernels, attend(): pl.pallas_call(attend_kernel, out_shape=(jax.ShapeDtypeStruct(query.shape...  26 us
  transfers between devices with their start and end apart: 3, of which 0 were waited for; matrix products, arithmetic and copies ran while one was open for 12% of the time, Pallas kernels for 48%

profile of v1, /device:TPU:0, one launch (start us, length us, event | category | flops | bytes accessed | tf_op | source)
XLA Modules:
  0.0 514.9 jit_solution(2618306481854813651)
XLA Ops:
  7.9 2.3 fusion.4
  10.7 0.7 concatenate.20.small_ref
  11.4 95.8 %gather_weights.1 = (bf16[32,48,2560]{2,1,0:T(8,128)(2,1)}, bf16[32,48,128]{2,1,0:T(8,128)(2,1)}, bf16[32,48,1536]{2,1,0:T(8,128)(2,1)}) custom-call(bf16[48,1536]{1,0:T(8,128)(2,1)} %query_ref.1, bf16[48,512]{1,0:T(8,128)(2,1)} %key_ref.1, bf16[48,512]{1,0:T(8,128)(2,1)} %value_ref.1, bf16[48,128]{1,0:T(8,128)(2,1)} %concatenate.20.small_ref, ...), custom_call_target="tpu_custom_call" | custom-call | tf_op jit(solution)/shard_map/gather_weights/pallas_call | solution.py:434
  107.3 1.7 convert_reduce_fusion
  109.0 0.2 fusion.13
  109.2 0.3 fusion.7
  109.5 6.6 %fusion.30 = f32[2560,256]{1,0:T(8,128)S(1)} fusion(bf16[1536,2560]{1,0:T(8,128)(2,1)} %bitcast.90, bf16[256,1536]{1,0:T(8,128)(2,1)S(1)} %fusion.7), kind=kOutput, calls=%fused_computation.76 | convolution fusion | flops 2013265920 | bytes 11272192 | tf_op jit(solution)/shard_map/de,sd->es/dot_general | solution.py:1712
  116.2 1.5 slice.79
  117.8 0.8 reshape.206.routes_ref
  118.6 0.8 copy.68
  119.6 2.0 add_convert_fusion
  121.8 26.0 %attend.1 = (bf16[1536,256]{1,0:T(8,128)(2,1)S(1)}, bf16[4,1024,256]{2,1,0:T(8,128)(2,1)S(1)}) custom-call(bf16[1536,256]{1,0:T(8,128)(2,1)S(1)} %bitcast.66, bf16[1024,256]{1,0:T(8,128)(2,1)S(1)} %pad_maximum_fusion.own_ref, s32[1]{0:T(128)} %copy.73.length_ref), custom_call_target="tpu_custom_call" | custom-call | tf_op jit(solution)/shard_map/attend/pallas_call | solution.py:797
  147.8 1.5 multiply_reduce_fusion.2
  149.4 1.1 copy-done.5
  150.5 1.1 multiply_convert_fusion.1.hidden_ref
  151.6 176.3 %experts.1 = (bf16[256,1536]{1,0:T(8,128)(2,1)}, bf16[16,256,1536]{2,1,0:T(8,128)(2,1)}, f32[16,8,256]{2,1,0:T(8,128)}, bf16[2,768,512]{2,1,0:T(8,128)(2,1)}, bf...) custom-call(bf16[256,1536]{1,0:T(8,128)(2,1)} %multiply_convert_fusi, ...), custom_call_target="tpu_custom_call" | custom-call | tf_op jit(solution)/shard_map/experts/pallas_call | solution.py:1594
  328.0 1.0 copy-done.8
  329.0 1.4 fusion.29
  330.4 0.9 slice.69
  331.4 2.0 multiply_reduce_fusion
  333.5 1.7 fusion.25
  335.2 1.6 collective-permute-start
  336.8 5.4 %convolution_convert_fusion.2.grad_ref = bf16[1536,256]{1,0:T(8,128)(2,1)} fusion(bf16[1536,1536]{1,0:T(8,128)(2,1)} %bitcast.70, bf16[256,1536]{1,0:T(8,128)(2,1)S(1)} %get-tuple-element.132), kind=kOutput, calls=%fused_computation.7 | convolution fusion | flops 1208352768 | bytes 6291456 | tf_op jit(solution)/shard_map/ed,sd->es/dot_general | solution.py:1759
  342.2 0.7 concatenate.28
  342.9 1.9 copy-done.3
  344.8 1.3 copy-done.4
  346.0 41.0 %attend_back.1 = bf16[2560,256]{1,0:T(8,128)(2,1)S(1)} custom-call(bf16[1536,256]{1,0:T(8,128)(2,1)S(1)} %bitcast.67, bf16[4,1024,256]{2,1,0:T(8,128)(2,1)S(1)} %copy-done.3, bf16[1536,256]{1,0:T(8,128)(2,1)S(1)} %copy-done.4, s32[1]{0:T(128)} %copy.73.length_ref, f32[32,256]{1,0:T(8,128)S(1)} %get-tuple-element.141.cosine_ref, ...), custom_call_target="tpu_custom_call" | custom-call | flops 1048576 | bytes 65536 | tf_op jit(solution)/shard_map/attend_back/pallas_call | solution.py:978
  387.1 6.9 %fusion.12 = (bf16[1536]{0:T(1024)(128)(2,1)S(1)}, f32[256]{0:T(256)S(1)}, f32[256,1536]{1,0:T(8,128)}) fusion(bf16[1,256,1536]{2,1,0:T(8,128)(2,1)S(1)} %copy-done.11, f32[256]{0:T(256)S(1)} %add_rsqrt_fusion.1, f32[1536]{0:T(1024)S(1)} %get-tuple-element.129, bf16[2560,256]{1,0:T(8,128)(2,1)S(1)} %attend_back.1, bf16[1536,2560]{1,0:T(8,128)(2,1)} %bitcast.91), kind=kOutput, calls=%fused_computation.25 | convolution fusion | flops 2016016640 | bytes 11545600 | tf_op jit(solution)/shard_map/es,de->sd/dot_general | solution.py:1763
  394.0 1.5 concatenate.27
  395.7 0.2 copy.64
  396.0 2.2 maximum_maximum_fusion.small_ref
  398.2 3.6 convolution_convert_fusion.1
  401.8 5.4 %convolution_convert_fusion = bf16[1536,2560]{1,0:T(8,128)(2,1)} fusion(bf16[256,1536]{1,0:T(8,128)(2,1)S(1)} %copy-done.16, bf16[2560,256]{1,0:T(8,128)(2,1)S(1)} %attend_back.1), kind=kOutput, calls=%fused_computation | convolution fusion | flops 2017198080 | bytes 9961472 | tf_op jit(solution)/shard_map/sd,es->de/dot_general | solution.py:1762
  407.2 1.6 fusion.11
  408.7 1.8 fusion.27
  410.5 1.6 fusion.28
  412.2 0.3 copy-done.20
  412.5 0.5 copy-done.21
  412.9 3.7 convert_add_fusion.1
  416.7 2.1 convert_add_fusion
  418.8 82.3 %sum_gradients.1 = (f32[48,1536]{1,0:T(8,128)}, f32[48,512]{1,0:T(8,128)}, f32[48,512]{1,0:T(8,128)}, f32[48,128]{1,0:T(8,128)}, f32[48,1536]{1,0:T(8,128)}) custom-call(bf16[2,16,48,2560]{3,2,1,0:T(8,128)(2,1)} %bitcast.68, bf16[2,16,48,128]{3,2,1,0:T(8,128)(2,1)} %maximum_maximum_fusion.small_ref, bf16[2,16,48,1536]{3,2,1,0:T(8,128)(2,1)} %bitcast.69), custom_call_target="tpu_custom_call" | custom-call | flops 1048576 | bytes 65536 | tf_op jit(solution)/shard_map/sum_gradients/pallas_call | solution.py:647
  501.2 2.3 fusion.16
  503.5 0.7 slice_reduce_fusion
  504.2 0.7 copy.67
  504.9 0.7 copy.74
  505.6 0.6 copy.75
  506.2 0.6 copy.76
  506.9 0.7 copy.77
  (104 shorter events, 1.7 us)
Async XLA Ops:
  7.2 3.1 copy-start.32
  7.2 3.2 copy-start.33
  7.2 3.3 copy-start.34
  7.2 3.4 copy-start.31
  7.2 144.4 %all-gather.2.cloned.1.call-start = ((), (), s32[]{:S(2)}) async-start(), calls=%async_computation.1 | async-start | bytes 13369344 | tf_op jit(solution)/shard_map/all_gather | solution.py:1702
  7.9 101.0 %copy-start.10 = (bf16[1,256,1536]{2,1,0:T(8,128)(2,1)S(1)}, bf16[1,256,1536]{2,1,0:T(8,128)(2,1)}, u32[]{:S(2)}) copy-start(bf16[1,256,1536]{2,1,0:T(8,128)(2,1)} %param.14) | copy-start | bytes 2359300
  10.2 490.9 %reduce-scatter.2.cloned.1.call-start = ((), (), s32[]{:S(2)}) async-start(), calls=%async_computation.2 | async-start | bytes 13369344 | tf_op jit(solution)/shard_map/reduce_scatter | solution.py:1728
  109.5 6.7 %copy-start.15 = (bf16[256,1536]{1,0:T(8,128)(2,1)}, bf16[256,1536]{1,0:T(8,128)(2,1)S(1)}, u32[]{:S(2)}) copy-start(bf16[256,1536]{1,0:T(8,128)(2,1)S(1)} %fusion.7) | copy-start | bytes 2359300
  116.1 1.5 copy-start.13
  116.1 31.7 %slice-start = ((s8[4718592]{0:T(1024)(128)(4,1)}), s8[524288]{0:T(1024)(128)(4,1)S(1)}, s32[]{:S(2)}) async-start(s8[4718592]{0:T(1024)(128)(4,1)} %bitcast.71), calls=%async_computation.3 | async-start | bytes 1048576
  119.6 28.2 %slice-start.1 = ((s8[4718592]{0:T(1024)(128)(4,1)}), s8[4194304]{0:T(1024)(128)(4,1)S(1)}, s32[]{:S(2)}) async-start(s8[4718592]{0:T(1024)(128)(4,1)} %bitcast.71), calls=%async_computation.4 | async-start | bytes 8388608
  121.8 27.5 %copy-start = (bf16[24,2,32,256]{3,2,1,0:T(8,128)(2,1)}, bf16[24,2,32,256]{3,2,1,0:T(8,128)(2,1)S(1)}, u32[]{:S(2)}) copy-start(bf16[24,2,32,256]{3,2,1,0:T(8,128)(2,1)S(1)} %fusion.15) | copy-start | bytes 2359300
  147.8 1.5 copy-start.2
  149.3 1.2 copy-start.5
  327.9 1.1 copy-start.8
  327.9 3.5 copy-start.6
  331.4 2.1 copy-start.19
  335.2 7.0 %copy-start.17 = (bf16[256,1536]{1,0:T(8,128)(2,1)}, bf16[256,1536]{1,0:T(8,128)(2,1)S(1)}, u32[]{:S(2)}) copy-start(bf16[256,1536]{1,0:T(8,128)(2,1)S(1)} %get-tuple-element.132) | copy-start | bytes 2359300
  335.2 7.7 %copy-start.1 = (bf16[24,2,32,256]{3,2,1,0:T(8,128)(2,1)S(1)}, bf16[24,2,32,256]{3,2,1,0:T(8,128)(2,1)}, u32[]{:S(2)}) copy-start(bf16[24,2,32,256]{3,2,1,0:T(8,128)(2,1)} %copy-done) | copy-start | bytes 2359300
  335.2 73.6 %collective-permute-start = (bf16[4,768,512]{2,1,0:T(8,128)(2,1)}, bf16[4,768,512]{2,1,0:T(8,128)(2,1)}, u32[]{:S(2)}, u32[]{:S(2)}) collective-permute-start(bf16[4,768,512]{2,1,0:T(8,128)(2,1)} %get-tuple-element.48), channel_id=1, source_target_pairs={{0,16},{16,0},{1,17},{17,1},{2,18},{18,2},{3,19},{19,3},{4,20},{20... | collective-permute-start | bytes 9437192 | tf_op jit(solution)/shard_map/ppermute | solution.py:1731
  342.9 1.9 copy-start.3
  344.8 1.3 copy-start.4
  346.0 41.0 %copy-start.11 = (bf16[1,256,1536]{2,1,0:T(8,128)(2,1)S(1)}, bf16[1,256,1536]{2,1,0:T(8,128)(2,1)}, u32[]{:S(2)}) copy-start(bf16[1,256,1536]{2,1,0:T(8,128)(2,1)} %param.14) | copy-start | bytes 2359300
  387.1 8.4 %copy-start.9 = (bf16[256,1536]{1,0:T(8,128)(2,1)S(1)}, bf16[256,1536]{1,0:T(8,128)(2,1)}, u32[]{:S(2)}) copy-start(bf16[256,1536]{1,0:T(8,128)(2,1)} %multiply_convert_fusion.1.hidden_ref) | copy-start | bytes 2359300
  395.9 2.2 copy-start.18
  398.2 3.6 copy-start.16
  401.8 5.4 %copy-start.12 = (bf16[1,256,1536]{2,1,0:T(8,128)(2,1)S(1)}, bf16[1,256,1536]{2,1,0:T(8,128)(2,1)}, u32[]{:S(2)}) copy-start(bf16[1,256,1536]{2,1,0:T(8,128)(2,1)} %param.14) | copy-start | bytes 2359300
  401.8 5.4 %copy-start.14 = (f32[256,1536]{1,0:T(8,128)S(1)}, f32[256,1536]{1,0:T(8,128)}, u32[]{:S(2)}) copy-start(f32[256,1536]{1,0:T(8,128)} %get-tuple-element.133) | copy-start | bytes 4718596
  401.8 5.4 %copy-start.23 = (f32[256,1536]{1,0:T(8,128)S(1)}, f32[256,1536]{1,0:T(8,128)}, u32[]{:S(2)}) copy-start(f32[256,1536]{1,0:T(8,128)} %get-tuple-element.148) | copy-start | bytes 4718596
  408.7 3.4 copy-start.24
  408.7 3.4 copy-start.25
  410.5 1.9 copy-start.20
  410.5 2.4 copy-start.21
  412.9 3.7 copy-start.22
  418.8 82.3 %copy-start.7 = (f32[256,1536]{1,0:T(8,128)S(1)}, f32[256,1536]{1,0:T(8,128)}, u32[]{:S(2)}) copy-start(f32[256,1536]{1,0:T(8,128)} %copy-done.5) | copy-start | bytes 4718596
  501.1 2.4 copy-start.28
  501.1 3.7 copy-start.27
  501.1 4.4 copy-start.30
  501.2 5.1 copy-start.29
  501.2 5.7 %copy-start.26 = (f32[48,1536]{1,0:T(8,128)S(1)}, f32[48,1536]{1,0:T(8,128)}, u32[]{:S(2)}) copy-start(f32[48,1536]{1,0:T(8,128)} %get-tuple-element.169) | copy-start | bytes 884740
Sparse Core Ops, SparseCore 0:
  10.9 116.3 all-gather.1
  328.0 145.1 reduce-scatter.1
